TPU v7x, 256 devices: a whole 4x4x8 slice. The times are simulated.
256 devices in a mesh: gx: 16 (over y_lo, z), gy: 16 (over x, y_hi, core).
Axes of the slice: x: 4, y: 4 (y_hi: 2, y_lo: 2; y = y_hi * 2 + y_lo), z: 8, core: 2. Of those that a mesh axis runs over, the one named last changes fastest.
Arguments:
- density: float32 [2, 256, 2048], P(None, 'gx', 'gy'), may hold values from 0.5 to 2
- momentum: float32 [3, 2, 256, 2048], P(None, None, 'gx', 'gy'), may hold values from -1.2 to 1.2
- field: float32 [3, 2, 256, 2048], P(None, None, 'gx', 'gy'), may hold values from -2 to 2
- fargo_offsets: int32 [2, 256], P(None, 'gx'), may hold values from 0 to 2047
- shear_shift: int32 [2], replicated, may hold values from 0 to 2047
Outputs:
- new_density: float32 [2, 256, 2048], P(None, 'gx', 'gy')
- new_momentum: float32 [3, 2, 256, 2048], P(None, None, 'gx', 'gy')
- new_field: float32 [3, 2, 256, 2048], P(None, None, 'gx', 'gy')
Inputs may be any that keep to these rules, and one draw needn't show every extreme that they name: `fargo_offsets`: column offsets are cell counts along the azimuth. `shear_shift`: the shift is held fixed within a step.
All inputs are finite; a program needn't handle non-finite values.
Results may differ from a plain program's by a relative error of at most 0.00002.
Values sent between devices are 32-bit elements; how exact they have to be, the bound alone decides.
No kernel may reach another device: no remote copies, remote signals or barrier semaphores. Data moves between devices by JAX's collectives and lax.ppermute only.
A program may use at most 64 MiB of HBM per device.

v0:
```python
import functools

import jax
import jax.numpy as jnp
from jax import lax
from jax.experimental import pallas as pl
from jax.experimental.pallas import tpu as pltpu
from jax.sharding import PartitionSpec as P

time_step = 0.03
rotation = 1.0
shear_rate = 1.5

ROWS = 16
LANES = 128
PARTS = 16
LEVELS = 2
SLABS = 14
BELOW = 5
ABOVE = 4
FULL = 9
LOW_ROWS = 72
UP_ROWS = 64


def slab(density, momentum, field, index):
    member, level = divmod(index, 2)
    if member == 0:
        return density[level]
    if member < 4:
        return momentum[member - 1, level]
    return field[member - 4, level]


def strip_kernel(density, momentum, field, offsets, low, up):
    low[...] = jnp.zeros_like(low)
    up[...] = jnp.zeros_like(up)
    for index in range(SLABS):
        rows = slab(density, momentum, field, index)
        low[pl.ds(index, BELOW, stride=SLABS), :] = rows[ROWS - BELOW :]
        up[pl.ds(index, ABOVE, stride=SLABS), :] = rows[:ABOVE]
    shifts = offsets[...].astype(jnp.float32)
    low[70:72, 0:ROWS] = shifts
    up[56:58, 0:ROWS] = shifts


def pack_kernel(density, momentum, field, low, up, send, ghost_offsets, rows_of):
    rows_of[0:70, :] = low[0:70, :]
    for index in range(SLABS):
        rows_of[pl.ds(BELOW * SLABS + index, ROWS, stride=SLABS), :] = slab(
            density, momentum, field, index
        )
    rows_of[294:350, :] = up[0:56, :]
    for part in range(PARTS):
        start = SLABS * (part + 1)
        send[part, 0:126, :] = rows_of[start : start + 126, :]
        start = SLABS * part + 8
        send[part, 126:128, :] = rows_of[start : start + 2, :]
    ghost_offsets[0:2, :] = low[70:72, :].astype(jnp.int32)
    ghost_offsets[2:4, :] = up[56:58, :].astype(jnp.int32)


def y_ahead(values, lane, sublane):
    turned = pltpu.roll(values, LANES - 1, 1)
    return jnp.where(lane == LANES - 1, pltpu.roll(turned, ROWS - 1, 0), turned)


def y_behind(values, lane, sublane):
    turned = pltpu.roll(values, 1, 1)
    return jnp.where(lane == 0, pltpu.roll(turned, 1, 0), turned)


def interface_flux(left, right, normal):
    rho_l, inv_l, vn_l, va_l, vb_l, mn_l, ma_l, mb_l, ba_l, bb_l = left
    rho_r, inv_r, vn_r, va_r, vb_r, mn_r, ma_r, mb_r, ba_r, bb_r = right
    normal_square = normal * normal
    square_l = ba_l * ba_l + bb_l * bb_l
    square_r = ba_r * ba_r + bb_r * bb_r
    arg_l = 1.0 + (normal_square + square_l) * inv_l
    arg_r = 1.0 + (normal_square + square_r) * inv_r
    signal_l = arg_l * lax.rsqrt(arg_l)
    signal_r = arg_r * lax.rsqrt(arg_r)
    lowest = jnp.minimum(jnp.minimum(vn_l - signal_l, vn_r - signal_r), 0.0)
    highest = jnp.maximum(jnp.maximum(vn_l + signal_l, vn_r + signal_r), 0.0)
    inverse = 1.0 / (highest - lowest)
    weight_l = highest * inverse
    weight_r = -lowest * inverse
    jump = lowest * weight_l

    def mix(flux_l, flux_r, cons_l, cons_r):
        return weight_l * flux_l + weight_r * flux_r + jump * (cons_r - cons_l)

    return (
        mix(mn_l, mn_r, rho_l, rho_r),
        mix(
            mn_l * vn_l + (rho_l + 0.5 * square_l),
            mn_r * vn_r + (rho_r + 0.5 * square_r),
            mn_l,
            mn_r,
        )
        - 0.5 * normal_square,
        mix(mn_l * va_l - normal * ba_l, mn_r * va_r - normal * ba_r, ma_l, ma_r),
        mix(mn_l * vb_l - normal * bb_l, mn_r * vb_r - normal * bb_r, mb_l, mb_r),
        mix(ba_l * vn_l - normal * va_l, ba_r * vn_r - normal * va_r, ba_l, ba_r),
        mix(bb_l * vn_l - normal * vb_l, bb_r * vn_r - normal * vb_r, bb_l, bb_r),
    )


def stage(count, source, base, base_skip, target, prim, fluxes, edges, lane):
    sublane = None
    ahead = lambda values: y_ahead(values, lane, sublane)
    behind = lambda values: y_behind(values, lane, sublane)

    def cells(row, carry):
        for z in range(2):
            rho = source[row, 0, z]
            inv = 1.0 / rho
            prim[row, 0, z] = inv
            prim[row, 1, z] = source[row, 1, z] * inv
            prim[row, 2, z] = source[row, 2, z] * inv
            prim[row, 3, z] = source[row, 3, z] * inv
            prim[row, 4, z] = 0.5 * (source[row, 4, z] + source[row - 1, 4, z])
            by = source[row, 5, z]
            prim[row, 5, z] = 0.5 * (by + behind(by))
            prim[row, 6, z] = 0.5 * (source[row, 6, z] + source[row, 6, 1 - z])
        return carry

    def side(row, z):
        rho = source[row, 0, z]
        momentum = [source[row, 1 + n, z] for n in range(3)]
        velocity = [prim[row, 1 + n, z] for n in range(3)]
        center = [prim[row, 4 + n, z] for n in range(3)]
        return rho, prim[row, 0, z], velocity, momentum, center

    def along(parts, n):
        rho, inv, velocity, momentum, center = parts
        a, b = (n + 1) % 3, (n + 2) % 3
        return (
            rho,
            inv,
            velocity[n],
            velocity[a],
            velocity[b],
            momentum[n],
            momentum[a],
            momentum[b],
            center[a],
            center[b],
        )

    def flux_x(row):
        for z in range(2):
            out = interface_flux(
                along(side(row, z), 0), along(side(row + 1, z), 0), source[row, 4, z]
            )
            for n in range(4):
                fluxes[row, n, z] = out[n]
            fluxes[row, 4, z] = out[4] + ahead(out[4])
            fluxes[row, 5, z] = out[5]

    def flux_y(row):
        for z in range(2):
            rho, inv, velocity, momentum, center = side(row, z)
            next_rho = ahead(rho)
            next_velocity = [ahead(v) for v in velocity]
            next_center = [ahead(center[0]), None, ahead(center[2])]
            shifted = (
                next_rho,
                1.0 / next_rho,
                next_velocity,
                [next_rho * v for v in next_velocity],
                next_center,
            )
            out = interface_flux(
                along((rho, inv, velocity, momentum, center), 1),
                along(shifted, 1),
                source[row, 5, z],
            )
            for n in range(4):
                fluxes[row, 6 + n, z] = out[n] - behind(out[n])
            fluxes[row, 10, z] = out[4]
            fluxes[row, 11, z] = out[5]

    def flux_z(row):
        for z in range(2):
            out = interface_flux(
                along(side(row, z), 2), along(side(row, 1 - z), 2), source[row, 6, z]
            )
            for n in range(4):
                fluxes[row, 12 + n, z] = out[n]
            fluxes[row, 16, z] = out[4]
            fluxes[row, 17, z] = out[5] + ahead(out[5])

    def inner(row, carry):
        flux_x(row)
        flux_y(row)
        flux_z(row)
        return carry

    def update(row, carry):
        edge_z, edge_x, edge_y = [], [], []
        for z in range(2):
            edge_z.append(
                0.25 * (fluxes[row, 11, z] + fluxes[row + 1, 11, z] - fluxes[row, 4, z])
            )
            edge_x.append(
                0.25 * (fluxes[row, 17, z] - fluxes[row, 10, z] - fluxes[row, 10, 1 - z])
            )
            edge_y.append(
                0.25
                * (
                    fluxes[row, 5, z]
                    + fluxes[row, 5, 1 - z]
                    - fluxes[row, 16, z]
                    - fluxes[row + 1, 16, z]
                )
            )
            edges[row, 0, z] = edge_z[z]
            edges[row, 1, z] = edge_y[z]

        def put(member, z, rate):
            value = source[row, member, z] + time_step * rate
            if base is not None:
                value = 0.5 * base[row + base_skip, member, z] + 0.5 * value
            target[row - 1, member, z] = value

        def diverge(z, nx, ny, nz):
            return (
                (fluxes[row, nx, z] - fluxes[row - 1, nx, z])
                + fluxes[row, 6 + ny, z]
                + (fluxes[row, 12 + nz, z] - fluxes[row, 12 + nz, 1 - z])
            )

        for z in range(2):
            put(0, z, -diverge(z, 0, 0, 0))
            put(1, z, 2.0 * rotation * source[row, 2, z] - diverge(z, 1, 3, 2))
            put(
                2,
                z,
                -diverge(z, 2, 1, 3) - (2.0 - shear_rate) * rotation * source[row, 1, z],
            )
            put(3, z, -diverge(z, 3, 2, 1))
            put(4, z, (edge_y[z] - edge_y[1 - z]) - (edge_z[z] - behind(edge_z[z])))
            put(5, z, (edge_z[z] - edges[row - 1, 0, z]) - (edge_x[z] - edge_x[1 - z]))
            put(6, z, (edge_x[z] - behind(edge_x[z])) - (edge_y[z] - edges[row - 1, 1, z]))
        return carry

    lax.fori_loop(1, count + 1, cells, 0)
    lax.fori_loop(1, count, inner, 0)
    flux_y(count)
    flux_z(count)
    lax.fori_loop(1, count, update, 0)


def rolled(twice, amount, lane):
    blocks = amount // LANES
    cells = amount % LANES
    here = pltpu.roll(twice[pl.ds(ROWS - blocks, ROWS), :], cells, 1)
    before = pltpu.roll(twice[pl.ds(ROWS - 1 - blocks, ROWS), :], cells, 1)
    return jnp.where(lane >= cells, here, before)


def advance_kernel(
    offsets, ghost_offsets, shear, place, received, send, state, first, prim, fluxes, edges, twice
):
    cycle = PARTS * LANES
    radial = place[0]
    own = place[1]
    radial_count = place[2]
    row_of = radial * ROWS + own
    total = radial_count * ROWS
    lane = lax.broadcasted_iota(jnp.int32, (ROWS, LANES), 1)

    def load(row, index):
        return received[pl.ds((row - 1) * SLABS + index, PARTS, stride=LANES), :]

    for z in range(2):
        state[0, 4, z] = received[pl.ds(126 + z, PARTS, stride=LANES), :]

    def fetch(row, carry):
        for index in range(SLABS):
            state[row, index // 2, index % 2] = load(row, index)
        return carry

    lax.fori_loop(1, FULL + 1, fetch, 0)

    def turn(ref, row, amount):
        for index in range(SLABS):
            values = ref[row, index // 2, index % 2]
            twice[index, 0:ROWS, :] = values
            twice[index, ROWS : 2 * ROWS, :] = values
        for index in range(SLABS):
            ref[row, index // 2, index % 2] = rolled(twice.at[index], amount, lane)

    def ghosts(row, carry):
        place_of = row_of - BELOW + row
        below = place_of < 0
        above = place_of >= total

        @pl.when(below | above)
        def _():
            shift = shear[0]
            turn(state, row, jnp.where(below, cycle - shift, shift) % cycle)

        return carry

    lax.fori_loop(0, FULL + 1, ghosts, 0)

    common = (prim, fluxes, edges, lane)
    stage(9, state, None, 0, first, *common)
    stage(7, first, state, 1, state, *common)

    def remap(row, carry):
        local = own - 3 + row
        below_offset = ghost_offsets[0, jnp.clip(local + ROWS, 0, ROWS - 1)]
        above_offset = ghost_offsets[2, jnp.clip(local - ROWS, 0, ROWS - 1)]
        own_offset = offsets[0, jnp.clip(local, 0, ROWS - 1)]
        offset = jnp.where(
            local < 0, below_offset, jnp.where(local >= ROWS, above_offset, own_offset)
        )
        place_of = row_of - 3 + row
        change = shear[1] - shear[0]
        amount = offset + jnp.where(
            place_of < 0, -change, jnp.where(place_of >= total, change, 0)
        )
        turn(state, row, (amount + 2 * cycle) % cycle)
        return carry

    lax.fori_loop(0, 6, remap, 0)

    stage(5, state, None, 0, first, *common)
    stage(3, first, state, 1, state, *common)

    turn(state, 1, offsets[1, own] % cycle)
    for index in range(SLABS):
        send[pl.ds(index, PARTS, stride=ROWS), :] = state[1, index // 2, index % 2]
    for index in range(SLABS, ROWS):
        send[pl.ds(index, PARTS, stride=ROWS), :] = jnp.zeros((PARTS, LANES), jnp.float32)


def unpack_kernel(received, density, momentum, field):
    for index in range(SLABS):
        rows = received[pl.ds(index, ROWS, stride=ROWS), :]
        member, level = divmod(index, 2)
        if member == 0:
            density[level] = rows
        elif member < 4:
            momentum[member - 1, level] = rows
        else:
            field[member - 4, level] = rows


def in_vmem(count):
    return [pl.BlockSpec(memory_space=pltpu.VMEM)] * count


def in_smem(count):
    return [pl.BlockSpec(memory_space=pltpu.SMEM)] * count


def f32(*shape):
    return jax.ShapeDtypeStruct(shape, jnp.float32)


params = pltpu.CompilerParams(vmem_limit_bytes=40 * 1024 * 1024)


def on_device(density, momentum, field, fargo_offsets, shear_shift):
    low, up = pl.pallas_call(
        strip_kernel,
        out_shape=(f32(LOW_ROWS, LANES), f32(UP_ROWS, LANES)),
        in_specs=in_vmem(4),
        out_specs=tuple(in_vmem(2)),
        compiler_params=params,
    )(density, momentum, field, fargo_offsets)
    count = lax.axis_size("gx")
    low = lax.ppermute(low, "gx", [(i, (i + 1) % count) for i in range(count)])
    up = lax.ppermute(up, "gx", [((i + 1) % count, i) for i in range(count)])
    send, ghost_offsets = pl.pallas_call(
        pack_kernel,
        out_shape=(f32(PARTS, LANES, LANES), jax.ShapeDtypeStruct((4, LANES), jnp.int32)),
        in_specs=in_vmem(5),
        out_specs=tuple(in_vmem(2)),
        scratch_shapes=[pltpu.VMEM((352, LANES), jnp.float32)],
        compiler_params=params,
    )(density, momentum, field, low, up)
    cycles = lax.all_to_all(send, "gy", split_axis=0, concat_axis=0, tiled=True)
    place = jnp.stack(
        [lax.axis_index("gx"), lax.axis_index("gy"), jnp.int32(count)]
    ).astype(jnp.int32)
    row = (2, ROWS, LANES)
    moved = pl.pallas_call(
        advance_kernel,
        out_shape=f32(PARTS * ROWS, LANES),
        in_specs=in_smem(4) + in_vmem(1),
        out_specs=in_vmem(1)[0],
        scratch_shapes=[
            pltpu.VMEM((FULL + 1, 7) + row, jnp.float32),
            pltpu.VMEM((FULL + 1, 7) + row, jnp.float32),
            pltpu.VMEM((FULL + 1, 7) + row, jnp.float32),
            pltpu.VMEM((FULL + 1, 18) + row, jnp.float32),
            pltpu.VMEM((FULL + 1, 2) + row, jnp.float32),
            pltpu.VMEM((SLABS, 2 * ROWS, LANES), jnp.float32),
        ],
        compiler_params=params,
    )(fargo_offsets, ghost_offsets, shear_shift, place, cycles.reshape(PARTS * LANES, LANES))
    moved = lax.all_to_all(
        moved.reshape(PARTS, ROWS, LANES), "gy", split_axis=0, concat_axis=0, tiled=True
    )
    return pl.pallas_call(
        unpack_kernel,
        out_shape=(f32(2, ROWS, LANES), f32(3, 2, ROWS, LANES), f32(3, 2, ROWS, LANES)),
        in_specs=in_vmem(1),
        out_specs=tuple(in_vmem(3)),
        compiler_params=params,
    )(moved.reshape(PARTS * ROWS, LANES))


def solution(mesh):
    placed = (
        P(None, "gx", "gy"),
        P(None, None, "gx", "gy"),
        P(None, None, "gx", "gy"),
        P(None, "gx"),
        P(),
    )
    return jax.shard_map(
        on_device,
        mesh=mesh,
        in_specs=placed,
        out_specs=(P(None, "gx", "gy"), P(None, None, "gx", "gy"), P(None, None, "gx", "gy")),
        check_vma=False,
    )
```

profile of v0, /device:TPU:1, one launch (start us, length us, event | category | flops | bytes accessed | tf_op | source)
XLA Modules:
  0.0 64.5 jit_solution(4155165856616869802)
XLA Ops:
  0.6 0.0 copy-start
  0.6 0.8 %copy-done = f32[3,2,16,128]{3,2,1,0:T(8,128)S(1)} copy-done((f32[3,2,16,128]{3,2,1,0:T(8,128)S(1)}, f32[3,2,16,128]{3,2,1,0:T(8,128)}, u32[]{:S(2)}) %copy-start) | copy-done | bytes 49176
  1.4 0.0 copy-start.1
  1.4 0.8 %copy-done.1 = f32[3,2,16,128]{3,2,1,0:T(8,128)S(1)} copy-done((f32[3,2,16,128]{3,2,1,0:T(8,128)S(1)}, f32[3,2,16,128]{3,2,1,0:T(8,128)}, u32[]{:S(2)}) %copy-start.1) | copy-done | bytes 49176
  2.2 0.0 copy-start.2
  2.2 0.7 %copy-done.2 = f32[2,16,128]{2,1,0:T(8,128)S(1)} copy-done((f32[2,16,128]{2,1,0:T(8,128)S(1)}, f32[2,16,128]{2,1,0:T(8,128)}, u32[]{:S(2)}) %copy-start.2) | copy-done | bytes 16408
  2.9 0.0 copy-start.3
  2.9 0.7 %copy-done.3 = s32[2,16]{1,0:T(2,128)S(1)} copy-done((s32[2,16]{1,0:T(2,128)S(1)}, s32[2,16]{1,0:T(2,128)}, u32[]{:S(2)}) %copy-start.3) | copy-done | bytes 152
  3.6 2.5 %collective-permute-start = (f32[72,128]{1,0:T(8,128)S(1)}, f32[72,128]{1,0:T(8,128)S(1)}, u32[]{:S(2)}, u32[]{:S(2)}) collective-permute-start(f32[72,128]{1,0:T(8,128)S(1)} %get-tuple-element.7), channel_id=1, source_target_pairs={{0,16},{16,32},{32,48},{48,64},{64,80},{80,96},{96,112},{112,128},... | collective-permute-start | bytes 110600 | tf_op jit(solution)/shard_map/ppermute | solution.py:377
  6.2 5.0 %collective-permute-start.1 = (f32[64,128]{1,0:T(8,128)S(1)}, f32[64,128]{1,0:T(8,128)S(1)}, u32[]{:S(2)}, u32[]{:S(2)}) collective-permute-start(f32[64,128]{1,0:T(8,128)S(1)} %get-tuple-element.8), channel_id=1, source_target_pairs={{16,0},{32,16},{48,32},{64,48},{80,64},{96,80},{112,96},{128,112},... | collective-permute-start | bytes 98312 | tf_op jit(solution)/shard_map/ppermute | solution.py:378
  11.2 1.0 %collective-permute-done.1.up = f32[64,128]{1,0:T(8,128)S(1)} collective-permute-done((f32[64,128]{1,0:T(8,128)S(1)}, f32[64,128]{1,0:T(8,128)S(1)}, u32[]{:S(2)}, u32[]{:S(2)}) %collective-permute-start.1) | collective-permute-done | bytes 32800 | tf_op jit(solution)/shard_map/ppermute | solution.py:378
  12.3 0.2 collective-permute-done.low
  12.5 1.1 %shard_map.77 = (f32[16,128,128]{2,1,0:T(8,128)}, s32[4,128]{1,0:T(4,128)S(1)}) custom-call(f32[2,16,128]{2,1,0:T(8,128)S(1)} %copy-done.2, f32[3,2,16,128]{3,2,1,0:T(8,128)S(1)} %copy-done, f32[3,2,16,128]{3,2,1,0:T(8,128)S(1)} %copy-done.1, f32[72,128]{1,0:T(8,128)S(1)} %collective-permute-done.low, f32[64,128]{1,0:T(8,128)S(1)} %collective-permute-done.1.up), custom_call_target="tpu_custom_call" | custom-call | tf_op jit(solution)/shard_map/pallas_call | solution.py:379
  13.5 8.2 %all-to-all-start = ((f32[16,128,128]{2,1,0:T(8,128)}), f32[16,128,128]{2,1,0:T(8,128)S(1)}, u32[]{:S(2)}, u32[]{:S(2)}) async-start(f32[16,128,128]{2,1,0:T(8,128)} %get-tuple-element.10), calls=%async_computation | async-start | bytes 2097152 | tf_op jit(solution)/shard_map/all_to_all | solution.py:387
  21.7 0.1 pad_add_fusion.place
  21.8 17.1 %all-to-all-done = f32[16,128,128]{2,1,0:T(8,128)S(1)} async-done(((f32[16,128,128]{2,1,0:T(8,128)}), f32[16,128,128]{2,1,0:T(8,128)S(1)}, u32[]{:S(2)}, u32[]{:S(2)}) %all-to-all-start) | async-done | bytes 1048608 | tf_op jit(solution)/shard_map/all_to_all | solution.py:387
  38.9 0.0 copy-start.4
  39.0 0.0 copy-start.5
  39.0 0.7 %copy-done.4 = s32[2,16]{1,0:T(2,128)S(1)} copy-done((s32[2,16]{1,0:T(2,128)S(1)}, s32[2,16]{1,0:T(2,128)}, u32[]{:S(2)}) %copy-start.4) | copy-done | bytes 152
  39.6 0.0 copy-done.5
  39.6 13.1 %shard_map.78 = f32[256,128]{1,0:T(8,128)S(1)} custom-call(s32[2,16]{1,0:T(2,128)S(1)} %copy-done.4, s32[4,128]{1,0:T(4,128)S(1)} %get-tuple-element.9.ghost_offsets, s32[2]{0:T(128)S(1)} %copy-done.5, s32[3]{0:T(128)S(1)} %pad_add_fusion.place, f32[2048,128]{1,0:T(8,128)S(1)} %bitcast.5), custom_call_target="tpu_custom_call" | custom-call | tf_op jit(solution)/shard_map/pallas_call | solution.py:392
  52.7 11.1 %all_to_all.10 = f32[16,16,128]{2,1,0:T(8,128)S(1)} all-to-all(f32[16,16,128]{2,1,0:T(8,128)S(1)} %bitcast.6), channel_id=1, replica_groups=mesh['gx'=16,'gy'=16] {'gy'}, dimensions={0} | all-to-all | bytes 262144 | tf_op jit(solution)/shard_map/all_to_all | solution.py:407
  63.8 0.7 %shard_map.79 = (f32[2,16,128]{2,1,0:T(8,128)}, f32[3,2,16,128]{3,2,1,0:T(8,128)}, f32[3,2,16,128]{3,2,1,0:T(8,128)}) custom-call(f32[256,128]{1,0:T(8,128)S(1)} %bitcast.7), custom_call_target="tpu_custom_call" | custom-call | tf_op jit(solution)/shard_map/pallas_call | solution.py:410
  (1 shorter events, 0.0 us)
Async XLA Ops:
  0.6 0.8 %copy-start = (f32[3,2,16,128]{3,2,1,0:T(8,128)S(1)}, f32[3,2,16,128]{3,2,1,0:T(8,128)}, u32[]{:S(2)}) copy-start(f32[3,2,16,128]{3,2,1,0:T(8,128)} %momentum.3) | copy-start | bytes 147460
  1.4 0.8 %copy-start.1 = (f32[3,2,16,128]{3,2,1,0:T(8,128)S(1)}, f32[3,2,16,128]{3,2,1,0:T(8,128)}, u32[]{:S(2)}) copy-start(f32[3,2,16,128]{3,2,1,0:T(8,128)} %field.3) | copy-start | bytes 147460
  2.2 0.7 %copy-start.2 = (f32[2,16,128]{2,1,0:T(8,128)S(1)}, f32[2,16,128]{2,1,0:T(8,128)}, u32[]{:S(2)}) copy-start(f32[2,16,128]{2,1,0:T(8,128)} %density.3) | copy-start | bytes 49156
  2.9 0.7 %copy-start.3 = (s32[2,16]{1,0:T(2,128)S(1)}, s32[2,16]{1,0:T(2,128)}, u32[]{:S(2)}) copy-start(s32[2,16]{1,0:T(2,128)} %offsets.3) | copy-start | bytes 388
  3.6 8.8 %collective-permute-start = (f32[72,128]{1,0:T(8,128)S(1)}, f32[72,128]{1,0:T(8,128)S(1)}, u32[]{:S(2)}, u32[]{:S(2)}) collective-permute-start(f32[72,128]{1,0:T(8,128)S(1)} %get-tuple-element.7), channel_id=1, source_target_pairs={{0,16},{16,32},{32,48},{48,64},{64,80},{80,96},{96,112},{112,128},... | collective-permute-start | bytes 110600 | tf_op jit(solution)/shard_map/ppermute | solution.py:377
  6.2 6.1 %collective-permute-start.1 = (f32[64,128]{1,0:T(8,128)S(1)}, f32[64,128]{1,0:T(8,128)S(1)}, u32[]{:S(2)}, u32[]{:S(2)}) collective-permute-start(f32[64,128]{1,0:T(8,128)S(1)} %get-tuple-element.8), channel_id=1, source_target_pairs={{16,0},{32,16},{48,32},{64,48},{80,64},{96,80},{112,96},{128,112},... | collective-permute-start | bytes 98312 | tf_op jit(solution)/shard_map/ppermute | solution.py:378
  13.5 25.4 %all-to-all-start = ((f32[16,128,128]{2,1,0:T(8,128)}), f32[16,128,128]{2,1,0:T(8,128)S(1)}, u32[]{:S(2)}, u32[]{:S(2)}) async-start(f32[16,128,128]{2,1,0:T(8,128)} %get-tuple-element.10), calls=%async_computation | async-start | bytes 2097152 | tf_op jit(solution)/shard_map/all_to_all | solution.py:387
  38.9 0.7 %copy-start.4 = (s32[2,16]{1,0:T(2,128)S(1)}, s32[2,16]{1,0:T(2,128)}, u32[]{:S(2)}) copy-start(s32[2,16]{1,0:T(2,128)} %offsets.3) | copy-start | bytes 388
  39.0 0.7 %copy-start.5 = (s32[2]{0:T(128)S(1)}, s32[2]{0:T(128)}, u32[]{:S(2)}) copy-start(s32[2]{0:T(128)} %shear.1) | copy-start | bytes 28
where the time goes:
time: 64.9 us; the launch traced here: 64.5 us
  waiting for transfers between devices  18.4 us (28%)
  starting transfers between devices  15.8 us (24%)
  Pallas kernels  14.8 us (23%)
  blocking collectives  11.1 us (17%)
  local copies, waits for them, and re-layouts  3.67 us (6%)
  between operations  0.66 us (1%)
    all_to_all x1, waiting for transfers between devices, on_device(): cycles = lax.all_to_all(send, 'gy', split_axis=0, concat_axis=0, tiled=True)  17.1 us
    pallas_call x1, Pallas kernels, on_device(): pl.pallas_call(advance_kernel, out_shape=f32(PARTS * ROWS, LANES), in_spe...  13.1 us
    all_to_all x1, blocking collectives, on_device(): lax.all_to_all(moved.reshape(PARTS, ROWS, LANES), 'gy', split_axis=0, con...  11.1 us
    all_to_all x1, starting transfers between devices, on_device(): cycles = lax.all_to_all(send, 'gy', split_axis=0, concat_axis=0, tiled=True)  8.19 us
    ppermute x1, starting transfers between devices, on_device(): up = lax.ppermute(up, 'gx', [((i + 1) % count, i) for i in range(count)])  5.04 us
    unnamed x12, local copies, waits for them, and re-layouts  3.67 us
    ppermute x1, starting transfers between devices, on_device(): low = lax.ppermute(low, 'gx', [(i, (i + 1) % count) for i in range(count)])  2.54 us
  transfers between devices with their start and end apart: 3, of which 3 were waited for; matrix products, arithmetic and copies ran while one was open for 0% of the time, Pallas kernels for 0%

commit v1 on v0

v1 whole, which is shorter than its diff:
```python
import functools

import jax
import jax.numpy as jnp
from jax import lax
from jax.experimental import pallas as pl
from jax.experimental.pallas import tpu as pltpu
from jax.sharding import PartitionSpec as P

time_step = 0.03
rotation = 1.0
shear_rate = 1.5

ROWS = 16
LANES = 128
PARTS = 16
LEVELS = 2
SLABS = 14
BELOW = 5
ABOVE = 4
FULL = 9
LOW_ROWS = 72
UP_ROWS = 64


def strip_kernel(held, low, up):
    for index in range(SLABS):
        rows = held[index]
        low[pl.ds(index, BELOW, stride=SLABS), :] = rows[ROWS - BELOW :]
        up[pl.ds(index, ABOVE, stride=SLABS), :] = rows[:ABOVE]
    low[70:72, :] = held[SLABS, 0:2, :]
    up[56:58, :] = held[SLABS, 0:2, :]
    up[58:64, :] = jnp.zeros((6, LANES), jnp.float32)


def pack_kernel(held, low, up, send, ghost_offsets, rows_of):
    rows_of[0:70, :] = low[0:70, :]
    for index in range(SLABS):
        rows_of[pl.ds(BELOW * SLABS + index, ROWS, stride=SLABS), :] = held[index]
    rows_of[294:350, :] = up[0:56, :]
    for part in range(PARTS):
        start = SLABS * (part + 1)
        send[part, 0:126, :] = rows_of[start : start + 126, :]
        start = SLABS * part + 8
        send[part, 126:128, :] = rows_of[start : start + 2, :]
    ghost_offsets[0:2, :] = low[70:72, :].astype(jnp.int32)
    ghost_offsets[2:4, :] = up[56:58, :].astype(jnp.int32)


def y_ahead(values, lane):
    turned = pltpu.roll(values, LANES - 1, 1)
    return jnp.where(lane == LANES - 1, pltpu.roll(turned, ROWS - 1, 0), turned)


def y_behind(values, lane):
    turned = pltpu.roll(values, 1, 1)
    return jnp.where(lane == 0, pltpu.roll(turned, 1, 0), turned)


def interface_flux(left, right, normal, along):
    rho_l, inv_l, v_l, c_l = left
    rho_r, inv_r, v_r, c_r = right
    one, two = (along + 1) % 3, (along + 2) % 3
    normal_square = normal * normal
    square_l = c_l[one] * c_l[one] + c_l[two] * c_l[two]
    square_r = c_r[one] * c_r[one] + c_r[two] * c_r[two]
    arg_l = 1.0 + (normal_square + square_l) * inv_l
    arg_r = 1.0 + (normal_square + square_r) * inv_r
    signal_l = arg_l * lax.rsqrt(arg_l)
    signal_r = arg_r * lax.rsqrt(arg_r)
    lowest = jnp.minimum(jnp.minimum(v_l[along] - signal_l, v_r[along] - signal_r), 0.0)
    highest = jnp.maximum(jnp.maximum(v_l[along] + signal_l, v_r[along] + signal_r), 0.0)
    inverse = 1.0 / (highest - lowest)
    weight_l = highest * inverse
    weight_r = lowest * inverse
    jump = lowest * weight_l
    pull_l = weight_l * v_l[along] - jump
    pull_r = jump - weight_r * v_r[along]
    mass_l = rho_l * pull_l
    mass_r = rho_r * pull_r
    line_l = weight_l * normal
    line_r = weight_r * normal
    pressure = weight_l * (rho_l + 0.5 * square_l) - weight_r * (rho_r + 0.5 * square_r)

    def carried(n):
        return mass_l * v_l[n] + mass_r * v_r[n]

    return (
        mass_l + mass_r,
        carried(along) + (pressure - 0.5 * normal_square),
        carried(one) - (line_l * c_l[one] - line_r * c_r[one]),
        carried(two) - (line_l * c_l[two] - line_r * c_r[two]),
        (pull_l * c_l[one] + pull_r * c_r[one]) - (line_l * v_l[one] - line_r * v_r[one]),
        (pull_l * c_l[two] + pull_r * c_r[two]) - (line_l * v_l[two] - line_r * v_r[two]),
    )


FX, FX_BY, FX_BZ = 0, 8, 10
DY, FY_BZ, FY_BX = 11, 19, 20
DZ, FZ_BX, FZ_BY = 22, 26, 28
FLUXES = 30


def stage(count, source, base, target, prim, fluxes, edges, lane):
    ahead = lambda values: y_ahead(values, lane)
    behind = lambda values: y_behind(values, lane)

    def cells(row, carry):
        for z in range(2):
            inv = 1.0 / source[row, 0, z]
            prim[row, 0, z] = inv
            for n in range(3):
                prim[row, 1 + n, z] = source[row, 1 + n, z] * inv
            by = source[row, 5, z]
            prim[row, 4, z] = 0.5 * (source[row, 4, z] + source[row - 1, 4, z])
            prim[row, 5, z] = 0.5 * (by + behind(by))
        mean = 0.5 * (source[row, 6, 0] + source[row, 6, 1])
        prim[row, 6, 0] = mean
        return carry

    def states(row):
        mean = prim[row, 6, 0]
        return [
            (
                source[row, 0, z],
                prim[row, 0, z],
                [prim[row, 1 + n, z] for n in range(3)],
                [prim[row, 4, z], prim[row, 5, z], mean],
            )
            for z in range(2)
        ]

    def flux_x(row, here, there):
        total = None
        for z in range(2):
            out = interface_flux(here[z], there[z], source[row, 4, z], 0)
            for n in range(4):
                fluxes[row, FX + 2 * n + z] = out[n]
            fluxes[row, FX_BY + z] = out[4] + ahead(out[4])
            total = out[5] if z == 0 else total + out[5]
        fluxes[row, FX_BZ] = total

    def flux_y(row, here):
        total = None
        for z in range(2):
            rho, _, velocity, center = here[z]
            rho = ahead(rho)
            shifted = (
                rho,
                1.0 / rho,
                [ahead(v) for v in velocity],
                [ahead(center[0]), None, ahead(center[2])],
            )
            out = interface_flux(here[z], shifted, source[row, 5, z], 1)
            for n in range(4):
                fluxes[row, DY + 2 * n + z] = out[n] - behind(out[n])
            fluxes[row, FY_BX + z] = out[5]
            total = out[4] if z == 0 else total + out[4]
        fluxes[row, FY_BZ] = total

    def flux_z(row, here):
        first = None
        for z in range(2):
            out = interface_flux(here[z], here[1 - z], source[row, 6, z], 2)
            if z == 0:
                first = out
            else:
                for n in range(4):
                    fluxes[row, DZ + n] = first[n] - out[n]
            fluxes[row, FZ_BX + z] = out[4]
            fluxes[row, FZ_BY + z] = out[5] + ahead(out[5])

    def inner(row, carry):
        here = states(row)
        flux_y(row, here)
        flux_z(row, here)
        flux_x(row, here, states(row + 1))
        return carry

    def update(row, carry):
        edge_x, edge_y, edge_z, around = [], [], [], []
        for z in range(2):
            edge_z.append(
                (fluxes[row, FY_BX + z] + fluxes[row + 1, FY_BX + z]) - fluxes[row, FX_BY + z]
            )
            edge_x.append(fluxes[row, FZ_BY + z] - fluxes[row, FY_BZ])
            around.append(fluxes[row, FZ_BX + z] + fluxes[row + 1, FZ_BX + z])
            edge_y.append(fluxes[row, FX_BZ] - around[z])
            edges[row, 0, z] = edge_z[z]
            edges[row, 1, z] = edge_y[z]
        turn_x = around[1] - around[0]
        turn_y = fluxes[row, FZ_BY] - fluxes[row, FZ_BY + 1]

        def put(member, z, value):
            if base is not None:
                value = 0.5 * (base[row + 1, member, z] + value)
            target[row - 1, member, z] = value

        def diverge(z, nx, ny, nz):
            here = fluxes[row, FX + 2 * nx + z] - fluxes[row - 1, FX + 2 * nx + z]
            here = here + fluxes[row, DY + 2 * ny + z]
            return here + fluxes[row, DZ + nz] if z == 0 else here - fluxes[row, DZ + nz]

        quarter = 0.25 * time_step
        for z in range(2):
            rho, mx, my, mz = (source[row, n, z] for n in range(4))
            put(0, z, rho - time_step * diverge(z, 0, 0, 0))
            put(1, z, mx + time_step * (2.0 * rotation * my - diverge(z, 1, 3, 2)))
            put(
                2,
                z,
                my - time_step * (diverge(z, 2, 1, 3) + (2.0 - shear_rate) * rotation * mx),
            )
            put(3, z, mz - time_step * diverge(z, 3, 2, 1))
            change = edge_z[z] - behind(edge_z[z])
            change = turn_x - change if z == 0 else -turn_x - change
            put(4, z, source[row, 4, z] + quarter * change)
            change = edge_z[z] - edges[row - 1, 0, z]
            change = change - turn_y if z == 0 else change + turn_y
            put(5, z, source[row, 5, z] + quarter * change)
            change = (edge_x[z] - behind(edge_x[z])) - (edge_y[z] - edges[row - 1, 1, z])
            put(6, z, source[row, 6, z] + quarter * change)
        return carry

    lax.fori_loop(1, count + 1, cells, 0, unroll=True)
    lax.fori_loop(1, count, inner, 0, unroll=2)
    last = states(count)
    flux_y(count, last)
    flux_z(count, last)
    lax.fori_loop(1, count, update, 0, unroll=True)


def rolled(twice, amount, lane):
    blocks = amount // LANES
    cells = amount % LANES
    here = pltpu.roll(twice[pl.ds(ROWS - blocks, ROWS), :], cells, 1)
    before = pltpu.roll(twice[pl.ds(ROWS - 1 - blocks, ROWS), :], cells, 1)
    return jnp.where(lane >= cells, here, before)


def advance_kernel(
    scalars,
    ghost_offsets,
    received,
    send,
    state,
    first,
    prim,
    fluxes,
    edges,
    twice,
):
    cycle = PARTS * LANES
    radial = scalars[0]
    own = scalars[1]
    radial_count = scalars[2]
    row_of = radial * ROWS + own
    total = radial_count * ROWS
    lane = lax.broadcasted_iota(jnp.int32, (ROWS, LANES), 1)

    def load(row, index):
        return received[pl.ds((row - 1) * SLABS + index, PARTS, stride=LANES), :]

    for z in range(2):
        state[0, 4, z] = received[pl.ds(126 + z, PARTS, stride=LANES), :]

    def fetch(row, carry):
        for index in range(SLABS):
            state[row, index // 2, index % 2] = load(row, index)
        return carry

    lax.fori_loop(1, FULL + 1, fetch, 0)

    def turn(ref, row, amount):
        for index in range(SLABS):
            values = ref[row, index // 2, index % 2]
            twice[index, 0:ROWS, :] = values
            twice[index, ROWS : 2 * ROWS, :] = values
        for index in range(SLABS):
            ref[row, index // 2, index % 2] = rolled(twice.at[index], amount, lane)

    def ghosts(row, carry):
        place_of = row_of - BELOW + row
        below = place_of < 0
        above = place_of >= total

        @pl.when(below | above)
        def _():
            shift = scalars[3]
            turn(state, row, jnp.where(below, cycle - shift, shift) % cycle)

        return carry

    lax.fori_loop(0, FULL + 1, ghosts, 0)

    common = (prim, fluxes, edges, lane)
    stage(9, state, None, first, *common)
    stage(7, first, state, state, *common)

    def remap(row, carry):
        local = own - 3 + row
        below_offset = ghost_offsets[0, jnp.clip(local + ROWS, 0, ROWS - 1)]
        above_offset = ghost_offsets[2, jnp.clip(local - ROWS, 0, ROWS - 1)]
        own_offset = scalars[5 + jnp.clip(local, 0, ROWS - 1)]
        offset = jnp.where(
            local < 0, below_offset, jnp.where(local >= ROWS, above_offset, own_offset)
        )
        place_of = row_of - 3 + row
        change = scalars[4] - scalars[3]
        amount = offset + jnp.where(
            place_of < 0, -change, jnp.where(place_of >= total, change, 0)
        )
        turn(state, row, (amount + 2 * cycle) % cycle)
        return carry

    lax.fori_loop(0, 6, remap, 0, unroll=True)

    stage(5, state, None, first, *common)
    stage(3, first, state, state, *common)

    turn(state, 1, scalars[5 + ROWS + own] % cycle)
    for index in range(SLABS):
        send[pl.ds(index, PARTS, stride=ROWS), :] = state[1, index // 2, index % 2]
    for index in range(SLABS, ROWS):
        send[pl.ds(index, PARTS, stride=ROWS), :] = jnp.zeros((PARTS, LANES), jnp.float32)


def unpack_kernel(received, density, momentum, field):
    for index in range(SLABS):
        rows = received[pl.ds(index, ROWS, stride=ROWS), :]
        member, level = divmod(index, 2)
        if member == 0:
            density[level] = rows
        elif member < 4:
            momentum[member - 1, level] = rows
        else:
            field[member - 4, level] = rows


def in_vmem(count):
    return [pl.BlockSpec(memory_space=pltpu.VMEM)] * count


def in_smem(count):
    return [pl.BlockSpec(memory_space=pltpu.SMEM)] * count


def f32(*shape):
    return jax.ShapeDtypeStruct(shape, jnp.float32)


params = pltpu.CompilerParams(vmem_limit_bytes=16 * 1024 * 1024)


def scratch():
    row = (2, ROWS, LANES)
    return [
        pltpu.VMEM((FULL + 1, 7) + row, jnp.float32),
        pltpu.VMEM((FULL + 1, 7) + row, jnp.float32),
        pltpu.VMEM((FULL + 1, 7) + row, jnp.float32),
        pltpu.VMEM((FULL + 1, FLUXES, ROWS, LANES), jnp.float32),
        pltpu.VMEM((FULL + 1, 2) + row, jnp.float32),
        pltpu.VMEM((SLABS, 2 * ROWS, LANES), jnp.float32),
    ]


def on_device(density, momentum, field, fargo_offsets, shear_shift):
    shifts = jnp.pad(fargo_offsets, ((0, ROWS - LEVELS), (0, LANES - ROWS))).astype(jnp.float32)
    block = (-1, ROWS, LANES)
    held = jnp.concatenate(
        [density, momentum.reshape(block), field.reshape(block), shifts[None]], axis=0
    )
    low, up = pl.pallas_call(
        strip_kernel,
        out_shape=(f32(LOW_ROWS, LANES), f32(UP_ROWS, LANES)),
        in_specs=in_vmem(1),
        out_specs=tuple(in_vmem(2)),
        compiler_params=params,
    )(held)
    count = lax.axis_size("gx")
    low = lax.ppermute(low, "gx", [(i, (i + 1) % count) for i in range(count)])
    up = lax.ppermute(up, "gx", [((i + 1) % count, i) for i in range(count)])
    place = jnp.stack([lax.axis_index("gx"), lax.axis_index("gy"), jnp.int32(count)])
    scalars = jnp.concatenate(
        [place.astype(jnp.int32), shear_shift, fargo_offsets.reshape(LEVELS * ROWS)]
    )
    low, up, scalars = lax.optimization_barrier((low, up, scalars))
    send, ghost_offsets = pl.pallas_call(
        pack_kernel,
        out_shape=(f32(PARTS, LANES, LANES), jax.ShapeDtypeStruct((4, LANES), jnp.int32)),
        in_specs=in_vmem(3),
        out_specs=tuple(in_vmem(2)),
        scratch_shapes=[pltpu.VMEM((352, LANES), jnp.float32)],
        compiler_params=params,
    )(held, low, up)
    cycles = lax.all_to_all(send, "gy", split_axis=0, concat_axis=0, tiled=True)
    moved = pl.pallas_call(
        advance_kernel,
        out_shape=f32(PARTS * ROWS, LANES),
        in_specs=in_smem(2) + in_vmem(1),
        out_specs=in_vmem(1)[0],
        scratch_shapes=scratch(),
        compiler_params=params,
    )(scalars, ghost_offsets, cycles.reshape(PARTS * LANES, LANES))
    moved = lax.all_to_all(
        moved.reshape(PARTS, ROWS, LANES), "gy", split_axis=0, concat_axis=0, tiled=True
    )
    return pl.pallas_call(
        unpack_kernel,
        out_shape=(f32(2, ROWS, LANES), f32(3, 2, ROWS, LANES), f32(3, 2, ROWS, LANES)),
        in_specs=in_vmem(1),
        out_specs=tuple(in_vmem(3)),
        compiler_params=params,
    )(moved.reshape(PARTS * ROWS, LANES))


def solution(mesh):
    placed = (
        P(None, "gx", "gy"),
        P(None, None, "gx", "gy"),
        P(None, None, "gx", "gy"),
        P(None, "gx"),
        P(),
    )
    return jax.shard_map(
        on_device,
        mesh=mesh,
        in_specs=placed,
        out_specs=(P(None, "gx", "gy"), P(None, None, "gx", "gy"), P(None, None, "gx", "gy")),
        check_vma=False,
    )
```

time: 64.9 us -> 55.8 us (0.86)
  blocking collectives: 11.1 us -> 36.3 us
  waiting for transfers between devices: 18.4 us -> 0.43 us
  starting transfers between devices: 15.8 us -> 7.59 us
  Pallas kernels: 14.8 us -> 8.22 us
  local copies, waits for them, and re-layouts: 3.67 us -> 0.81 us
  other arithmetic: 0.08 us -> 1.52 us
    all_to_all x0 -> x1, blocking collectives: none -> 24.7 us  [on_device(): cycles = lax.all_to_all(send, 'gy', split_axis=0, concat_axis=0, tiled=True)]
    all_to_all x1 -> x0, waiting for transfers between devices: 17.1 us -> none  [on_device(): cycles = lax.all_to_all(send, 'gy', split_axis=0, concat_axis=0, tiled=True)]
    all_to_all x1 -> x0, starting transfers between devices: 8.19 us -> none  [on_device(): cycles = lax.all_to_all(send, 'gy', split_axis=0, concat_axis=0, tiled=True)]
    pallas_call x1, Pallas kernels: 13.1 us -> 7.44 us  [on_device(): pl.pallas_call(advance_kernel, out_shape=f32(PARTS * ROWS, LANES), in_spe...]
    unnamed x12 -> x4, local copies, waits for them, and re-layouts: 3.67 us -> 0.66 us
    pallas_call x1, Pallas kernels: 1.06 us -> 0.09 us  [on_device(): pl.pallas_call(pack_kernel, out_shape=(f32(PARTS, LANES, LANES), jax.Shap...]
    concatenate x0 -> x1, other arithmetic: none -> 0.83 us  [on_device(): jnp.concatenate([density, momentum.reshape(block), field.reshape(block),...]
    ppermute x1, waiting for transfers between devices: 1.02 us -> 0.21 us  [on_device(): up = lax.ppermute(up, 'gx', [((i + 1) % count, i) for i in range(count)])]
  transfers between devices with their start and end apart: 3 -> 2, of which waited for: 3 -> 2; matrix products, arithmetic and copies ran while one was open for 0% -> 0% of each run, Pallas kernels for 0% -> 0%
where the time goes in v1:
time: 55.8 us; the launch traced here: 55.6 us
  blocking collectives  36.3 us (65%)
  Pallas kernels  8.22 us (15%)
  starting transfers between devices  7.59 us (14%)
  other arithmetic  1.52 us (3%)
  local copies, waits for them, and re-layouts  0.81 us (1%)
  between operations  0.66 us (1%)
    all_to_all x1, blocking collectives, on_device(): cycles = lax.all_to_all(send, 'gy', split_axis=0, concat_axis=0, tiled=True)  24.7 us
    all_to_all x1, blocking collectives, on_device(): lax.all_to_all(moved.reshape(PARTS, ROWS, LANES), 'gy', split_axis=0, con...  11.6 us
    pallas_call x1, Pallas kernels, on_device(): pl.pallas_call(advance_kernel, out_shape=f32(PARTS * ROWS, LANES), in_spe...  7.44 us
    ppermute x1, starting transfers between devices, on_device(): up = lax.ppermute(up, 'gx', [((i + 1) % count, i) for i in range(count)])  5.05 us
    ppermute x1, starting transfers between devices, on_device(): low = lax.ppermute(low, 'gx', [(i, (i + 1) % count) for i in range(count)])  2.54 us
  transfers between devices with their start and end apart: 2, of which 2 were waited for; matrix products, arithmetic and copies ran while one was open for 0% of the time, Pallas kernels for 0%

profile of v1, /device:TPU:1, one launch (start us, length us, event | category | flops | bytes accessed | tf_op | source)
XLA Modules:
  0.0 55.6 jit_solution(11688187982240362563)
XLA Ops:
  0.6 0.7 %convert_bitcast_fusion = f32[1,16,128]{2,1,0:T(8,128)S(1)} fusion(s32[2,16]{1,0:T(2,128)} %param.8), kind=kLoop, calls=%fused_computation.1 | loop fusion | flops 2048 | bytes 8320 | tf_op jit(solution)/shard_map/broadcast_in_dim | solution.py:371
  1.3 0.8 %pad_maximum_fusion.held = f32[15,16,128]{2,1,0:T(8,128)S(1)} fusion(f32[1,16,128]{2,1,0:T(8,128)S(1)} %convert_bitcast_fusion, f32[6,16,128]{2,1,0:T(8,128)} %bitcast.12, f32[6,16,128]{2,1,0:T(8,128)} %bitcast.13, f32[2,16,128]{2,1,0:T(8,128)} %param.5), kind=kLoop, calls=%fused_computation | loop fusion | flops 92160 | bytes 245760 | tf_op jit(solution)/shard_map/concatenate | solution.py:370
  2.2 2.5 %collective-permute-start = (f32[72,128]{1,0:T(8,128)S(1)}, f32[72,128]{1,0:T(8,128)S(1)}, u32[]{:S(2)}, u32[]{:S(2)}) collective-permute-start(f32[72,128]{1,0:T(8,128)S(1)} %get-tuple-element.10), channel_id=1, source_target_pairs={{0,16},{16,32},{32,48},{48,64},{64,80},{80,96},{96,112},{112,128},... | collective-permute-start | bytes 110600 | tf_op jit(solution)/shard_map/ppermute | solution.py:381
  4.7 0.0 copy-start
  4.7 5.1 %collective-permute-start.1 = (f32[64,128]{1,0:T(8,128)S(1)}, f32[64,128]{1,0:T(8,128)S(1)}, u32[]{:S(2)}, u32[]{:S(2)}) collective-permute-start(f32[64,128]{1,0:T(8,128)S(1)} %get-tuple-element.11), channel_id=1, source_target_pairs={{16,0},{32,16},{48,32},{64,48},{80,64},{96,80},{112,96},{128,112},... | collective-permute-start | bytes 98312 | tf_op jit(solution)/shard_map/ppermute | solution.py:382
  9.8 0.0 copy-done
  9.8 0.1 reshape.26
  9.9 0.0 copy-start.1
  9.9 0.7 %copy-done.1 = s32[2]{0:T(128)S(1)} copy-done((s32[2]{0:T(128)S(1)}, s32[2]{0:T(128)}, u32[]{:S(2)}) %copy-start.1) | copy-done | bytes 32
  10.5 0.1 concatenate.7.scalars
  10.6 0.2 collective-permute-done.1.up
  10.8 0.2 collective-permute-done.low
  11.0 0.1 shard_map.77
  11.1 24.7 %all_to_all.10 = f32[16,128,128]{2,1,0:T(8,128)S(1)} all-to-all(f32[16,128,128]{2,1,0:T(8,128)S(1)} %get-tuple-element.16), channel_id=1, replica_groups=mesh['gx'=16,'gy'=16] {'gy'}, dimensions={0} | all-to-all | bytes 2097152 | tf_op jit(solution)/shard_map/all_to_all | solution.py:396
  35.8 7.4 %shard_map.78 = f32[256,128]{1,0:T(8,128)S(1)} custom-call(s32[37]{0:T(128)S(1)} %concatenate.7.scalars, s32[4,128]{1,0:T(4,128)S(1)} %get-tuple-element.15.ghost_offsets, f32[2048,128]{1,0:T(8,128)S(1)} %bitcast.9), custom_call_target="tpu_custom_call" | custom-call | tf_op jit(solution)/shard_map/pallas_call | solution.py:397
  43.3 11.6 %all_to_all.11 = f32[16,16,128]{2,1,0:T(8,128)S(1)} all-to-all(f32[16,16,128]{2,1,0:T(8,128)S(1)} %bitcast.10), channel_id=1, replica_groups=mesh['gx'=16,'gy'=16] {'gy'}, dimensions={0} | all-to-all | bytes 262144 | tf_op jit(solution)/shard_map/all_to_all | solution.py:405
  54.9 0.7 %shard_map.79 = (f32[2,16,128]{2,1,0:T(8,128)}, f32[3,2,16,128]{3,2,1,0:T(8,128)}, f32[3,2,16,128]{3,2,1,0:T(8,128)}) custom-call(f32[256,128]{1,0:T(8,128)S(1)} %bitcast.11), custom_call_target="tpu_custom_call" | custom-call | tf_op jit(solution)/shard_map/pallas_call | solution.py:408
  (1 shorter events, 0.0 us)
Async XLA Ops:
  2.2 8.8 %collective-permute-start = (f32[72,128]{1,0:T(8,128)S(1)}, f32[72,128]{1,0:T(8,128)S(1)}, u32[]{:S(2)}, u32[]{:S(2)}) collective-permute-start(f32[72,128]{1,0:T(8,128)S(1)} %get-tuple-element.10), channel_id=1, source_target_pairs={{0,16},{16,32},{32,48},{48,64},{64,80},{80,96},{96,112},{112,128},... | collective-permute-start | bytes 110600 | tf_op jit(solution)/shard_map/ppermute | solution.py:381
  4.7 5.1 %copy-start = (s32[2,16]{1,0:T(2,128)S(1)}, s32[2,16]{1,0:T(2,128)}, u32[]{:S(2)}) copy-start(s32[2,16]{1,0:T(2,128)} %param.8) | copy-start | bytes 388
  4.7 6.1 %collective-permute-start.1 = (f32[64,128]{1,0:T(8,128)S(1)}, f32[64,128]{1,0:T(8,128)S(1)}, u32[]{:S(2)}, u32[]{:S(2)}) collective-permute-start(f32[64,128]{1,0:T(8,128)S(1)} %get-tuple-element.11), channel_id=1, source_target_pairs={{16,0},{32,16},{48,32},{64,48},{80,64},{96,80},{112,96},{128,112},... | collective-permute-start | bytes 98312 | tf_op jit(solution)/shard_map/ppermute | solution.py:382
  9.9 0.7 %copy-start.1 = (s32[2]{0:T(128)S(1)}, s32[2]{0:T(128)}, u32[]{:S(2)}) copy-start(s32[2]{0:T(128)} %param.9) | copy-start | bytes 28

commit v2 on v1

--- a/solution.py
+++ b/solution.py
@@ -14,6 +14,7 @@
 ROWS = 16
 LANES = 128
 PARTS = 16
+HALF = PARTS // 2
 LEVELS = 2
 SLABS = 14
 BELOW = 5
@@ -21,6 +22,7 @@
 FULL = 9
 LOW_ROWS = 72
 UP_ROWS = 64
+CHUNK = 144
 
 
 def strip_kernel(held, low, up):
@@ -38,23 +40,30 @@
     for index in range(SLABS):
         rows_of[pl.ds(BELOW * SLABS + index, ROWS, stride=SLABS), :] = held[index]
     rows_of[294:350, :] = up[0:56, :]
-    for part in range(PARTS):
-        start = SLABS * (part + 1)
-        send[part, 0:126, :] = rows_of[start : start + 126, :]
-        start = SLABS * part + 8
-        send[part, 126:128, :] = rows_of[start : start + 2, :]
+    for pair in range(HALF):
+        start = SLABS * (2 * pair + 1)
+        send[pair, 0:140, :] = rows_of[start : start + 140, :]
+        start = SLABS * (2 * pair) + 8
+        send[pair, 140:142, :] = rows_of[start : start + 2, :]
+        send[pair, 142:CHUNK, :] = jnp.zeros((CHUNK - 142, LANES), jnp.float32)
     ghost_offsets[0:2, :] = low[70:72, :].astype(jnp.int32)
     ghost_offsets[2:4, :] = up[56:58, :].astype(jnp.int32)
 
 
 def y_ahead(values, lane):
-    turned = pltpu.roll(values, LANES - 1, 1)
-    return jnp.where(lane == LANES - 1, pltpu.roll(turned, ROWS - 1, 0), turned)
+    turned = pltpu.roll(values, LANES - 1, 2)
+    even, odd = turned[0], turned[1]
+    last = lane == LANES - 1
+    return jnp.stack(
+        [jnp.where(last, odd, even), jnp.where(last, pltpu.roll(even, HALF - 1, 0), odd)]
+    )
 
 
 def y_behind(values, lane):
-    turned = pltpu.roll(values, 1, 1)
-    return jnp.where(lane == 0, pltpu.roll(turned, 1, 0), turned)
+    turned = pltpu.roll(values, 1, 2)
+    even, odd = turned[0], turned[1]
+    first = lane == 0
+    return jnp.stack([jnp.where(first, pltpu.roll(odd, 1, 0), even), jnp.where(first, even, odd)])
 
 
 def interface_flux(left, right, normal, along):
@@ -140,7 +149,7 @@
             total = out[5] if z == 0 else total + out[5]
         fluxes[row, FX_BZ] = total
 
-    def flux_y(row, here):
+    def flux_y(row, here, radial_only):
         total = None
         for z in range(2):
             rho, _, velocity, center = here[z]
@@ -152,44 +161,52 @@
                 [ahead(center[0]), None, ahead(center[2])],
             )
             out = interface_flux(here[z], shifted, source[row, 5, z], 1)
+            fluxes[row, FY_BX + z] = out[5]
+            if radial_only:
+                continue
             for n in range(4):
                 fluxes[row, DY + 2 * n + z] = out[n] - behind(out[n])
-            fluxes[row, FY_BX + z] = out[5]
             total = out[4] if z == 0 else total + out[4]
-        fluxes[row, FY_BZ] = total
-
-    def flux_z(row, here):
+        if not radial_only:
+            fluxes[row, FY_BZ] = total
+
+    def flux_z(row, here, radial_only):
         first = None
         for z in range(2):
             out = interface_flux(here[z], here[1 - z], source[row, 6, z], 2)
+            fluxes[row, FZ_BX + z] = out[4]
+            if radial_only:
+                continue
             if z == 0:
                 first = out
             else:
                 for n in range(4):
                     fluxes[row, DZ + n] = first[n] - out[n]
-            fluxes[row, FZ_BX + z] = out[4]
             fluxes[row, FZ_BY + z] = out[5] + ahead(out[5])
 
-    def inner(row, carry):
-        here = states(row)
-        flux_y(row, here)
-        flux_z(row, here)
-        flux_x(row, here, states(row + 1))
-        return carry
-
-    def update(row, carry):
+    def two_rows(row, opening):
+        one, two = states(row), states(row + 1)
+        flux_y(row, one, opening)
+        flux_z(row, one, opening)
+        flux_x(row, one, two)
+        three = states(row + 2)
+        flux_y(row + 1, two, False)
+        flux_z(row + 1, two, False)
+        flux_x(row + 1, two, three)
+
+    def update(row, radial_only):
         edge_x, edge_y, edge_z, around = [], [], [], []
         for z in range(2):
             edge_z.append(
                 (fluxes[row, FY_BX + z] + fluxes[row + 1, FY_BX + z]) - fluxes[row, FX_BY + z]
             )
-            edge_x.append(fluxes[row, FZ_BY + z] - fluxes[row, FY_BZ])
             around.append(fluxes[row, FZ_BX + z] + fluxes[row + 1, FZ_BX + z])
             edge_y.append(fluxes[row, FX_BZ] - around[z])
             edges[row, 0, z] = edge_z[z]
             edges[row, 1, z] = edge_y[z]
+            if not radial_only:
+                edge_x.append(fluxes[row, FZ_BY + z] - fluxes[row, FY_BZ])
         turn_x = around[1] - around[0]
-        turn_y = fluxes[row, FZ_BY] - fluxes[row, FZ_BY + 1]
 
         def put(member, z, value):
             if base is not None:
@@ -202,6 +219,13 @@
             return here + fluxes[row, DZ + nz] if z == 0 else here - fluxes[row, DZ + nz]
 
         quarter = 0.25 * time_step
+        for z in range(2):
+            change = edge_z[z] - behind(edge_z[z])
+            change = turn_x - change if z == 0 else -turn_x - change
+            put(4, z, source[row, 4, z] + quarter * change)
+        if radial_only:
+            return
+        turn_y = fluxes[row, FZ_BY] - fluxes[row, FZ_BY + 1]
         for z in range(2):
             rho, mx, my, mz = (source[row, n, z] for n in range(4))
             put(0, z, rho - time_step * diverge(z, 0, 0, 0))
@@ -212,36 +236,48 @@
                 my - time_step * (diverge(z, 2, 1, 3) + (2.0 - shear_rate) * rotation * mx),
             )
             put(3, z, mz - time_step * diverge(z, 3, 2, 1))
-            change = edge_z[z] - behind(edge_z[z])
-            change = turn_x - change if z == 0 else -turn_x - change
-            put(4, z, source[row, 4, z] + quarter * change)
             change = edge_z[z] - edges[row - 1, 0, z]
             change = change - turn_y if z == 0 else change + turn_y
             put(5, z, source[row, 5, z] + quarter * change)
             change = (edge_x[z] - behind(edge_x[z])) - (edge_y[z] - edges[row - 1, 1, z])
             put(6, z, source[row, 6, z] + quarter * change)
+
+    def more(pair, carry):
+        two_rows(2 * pair + 1, False)
         return carry
 
     lax.fori_loop(1, count + 1, cells, 0, unroll=True)
-    lax.fori_loop(1, count, inner, 0, unroll=2)
+    two_rows(1, True)
+    lax.fori_loop(1, (count - 1) // 2, more, 0)
     last = states(count)
-    flux_y(count, last)
-    flux_z(count, last)
-    lax.fori_loop(1, count, update, 0, unroll=True)
+    flux_y(count, last, True)
+    flux_z(count, last, True)
+    for row in range(1, count):
+        update(row, row == 1)
 
 
 def rolled(twice, amount, lane):
     blocks = amount // LANES
     cells = amount % LANES
-    here = pltpu.roll(twice[pl.ds(ROWS - blocks, ROWS), :], cells, 1)
-    before = pltpu.roll(twice[pl.ds(ROWS - 1 - blocks, ROWS), :], cells, 1)
-    return jnp.where(lane >= cells, here, before)
+    parts = []
+    for odd in range(2):
+        start = PARTS - blocks + odd
+        here = pltpu.roll(twice[pl.ds(start, HALF, stride=2), :], cells, 1)
+        before = pltpu.roll(twice[pl.ds(start - 1, HALF, stride=2), :], cells, 1)
+        parts.append(jnp.where(lane >= cells, here, before))
+    return jnp.stack(parts)
+
+
+def to_blocks(ref, start, stride, values):
+    for odd in range(2):
+        ref[pl.ds(start + odd * stride, HALF, stride=2 * stride), :] = values[odd]
 
 
 def advance_kernel(
     scalars,
     ghost_offsets,
-    received,
+    mine,
+    other,
     send,
     state,
     first,
@@ -256,28 +292,32 @@
     radial_count = scalars[2]
     row_of = radial * ROWS + own
     total = radial_count * ROWS
-    lane = lax.broadcasted_iota(jnp.int32, (ROWS, LANES), 1)
-
-    def load(row, index):
-        return received[pl.ds((row - 1) * SLABS + index, PARTS, stride=LANES), :]
+    lane = lax.broadcasted_iota(jnp.int32, (HALF, LANES), 1)
+
+    core = own % 2
+
+    def fetch_slab(row, member, z, start):
+        for parity, blocks in ((core, mine), (1 - core, other)):
+            state[row, member, z, parity] = blocks[pl.ds(start, HALF, stride=CHUNK), :]
 
     for z in range(2):
-        state[0, 4, z] = received[pl.ds(126 + z, PARTS, stride=LANES), :]
+        fetch_slab(0, 4, z, jnp.where(core == 0, 140, 8) + z)
 
     def fetch(row, carry):
         for index in range(SLABS):
-            state[row, index // 2, index % 2] = load(row, index)
+            fetch_slab(row, index // 2, index % 2, (row - 1 + core) * SLABS + index)
         return carry
 
     lax.fori_loop(1, FULL + 1, fetch, 0)
 
-    def turn(ref, row, amount):
-        for index in range(SLABS):
-            values = ref[row, index // 2, index % 2]
-            twice[index, 0:ROWS, :] = values
-            twice[index, ROWS : 2 * ROWS, :] = values
-        for index in range(SLABS):
-            ref[row, index // 2, index % 2] = rolled(twice.at[index], amount, lane)
+    def turn(ref, row, amount, members=range(7)):
+        slabs = [(member, z) for member in members for z in range(2)]
+        for place, (member, z) in enumerate(slabs):
+            values = ref[row, member, z]
+            to_blocks(twice.at[place], 0, 1, values)
+            to_blocks(twice.at[place], PARTS, 1, values)
+        for place, (member, z) in enumerate(slabs):
+            ref[row, member, z] = rolled(twice.at[place], amount, lane)
 
     def ghosts(row, carry):
         place_of = row_of - BELOW + row
@@ -297,7 +337,7 @@
     stage(9, state, None, first, *common)
     stage(7, first, state, state, *common)
 
-    def remap(row, carry):
+    def remap(row):
         local = own - 3 + row
         below_offset = ghost_offsets[0, jnp.clip(local + ROWS, 0, ROWS - 1)]
         above_offset = ghost_offsets[2, jnp.clip(local - ROWS, 0, ROWS - 1)]
@@ -310,17 +350,17 @@
         amount = offset + jnp.where(
             place_of < 0, -change, jnp.where(place_of >= total, change, 0)
         )
-        turn(state, row, (amount + 2 * cycle) % cycle)
-        return carry
-
-    lax.fori_loop(0, 6, remap, 0, unroll=True)
+        turn(state, row, (amount + 2 * cycle) % cycle, range(4, 5) if row == 0 else range(7))
+
+    for row in range(6):
+        remap(row)
 
     stage(5, state, None, first, *common)
     stage(3, first, state, state, *common)
 
     turn(state, 1, scalars[5 + ROWS + own] % cycle)
     for index in range(SLABS):
-        send[pl.ds(index, PARTS, stride=ROWS), :] = state[1, index // 2, index % 2]
+        to_blocks(send, index, ROWS, state[1, index // 2, index % 2])
     for index in range(SLABS, ROWS):
         send[pl.ds(index, PARTS, stride=ROWS), :] = jnp.zeros((PARTS, LANES), jnp.float32)
 
@@ -353,12 +393,12 @@
 
 
 def scratch():
-    row = (2, ROWS, LANES)
+    row = (2, 2, HALF, LANES)
     return [
         pltpu.VMEM((FULL + 1, 7) + row, jnp.float32),
         pltpu.VMEM((FULL + 1, 7) + row, jnp.float32),
         pltpu.VMEM((FULL + 1, 7) + row, jnp.float32),
-        pltpu.VMEM((FULL + 1, FLUXES, ROWS, LANES), jnp.float32),
+        pltpu.VMEM((FULL + 1, FLUXES, 2, HALF, LANES), jnp.float32),
         pltpu.VMEM((FULL + 1, 2) + row, jnp.float32),
         pltpu.VMEM((SLABS, 2 * ROWS, LANES), jnp.float32),
     ]
@@ -387,21 +427,26 @@
     low, up, scalars = lax.optimization_barrier((low, up, scalars))
     send, ghost_offsets = pl.pallas_call(
         pack_kernel,
-        out_shape=(f32(PARTS, LANES, LANES), jax.ShapeDtypeStruct((4, LANES), jnp.int32)),
+        out_shape=(f32(HALF, CHUNK, LANES), jax.ShapeDtypeStruct((4, LANES), jnp.int32)),
         in_specs=in_vmem(3),
         out_specs=tuple(in_vmem(2)),
         scratch_shapes=[pltpu.VMEM((352, LANES), jnp.float32)],
         compiler_params=params,
     )(held, low, up)
-    cycles = lax.all_to_all(send, "gy", split_axis=0, concat_axis=0, tiled=True)
+    alike = [list(range(core, PARTS, 2)) for core in range(2)]
+    mine = lax.all_to_all(
+        send, "gy", split_axis=0, concat_axis=0, tiled=True, axis_index_groups=alike
+    )
+    mine = mine.reshape(HALF * CHUNK, LANES)
+    other = lax.ppermute(mine, "gy", [(i, i ^ 1) for i in range(PARTS)])
     moved = pl.pallas_call(
         advance_kernel,
         out_shape=f32(PARTS * ROWS, LANES),
-        in_specs=in_smem(2) + in_vmem(1),
+        in_specs=in_smem(2) + in_vmem(2),
         out_specs=in_vmem(1)[0],
         scratch_shapes=scratch(),
         compiler_params=params,
-    )(scalars, ghost_offsets, cycles.reshape(PARTS * LANES, LANES))
+    )(scalars, ghost_offsets, mine, other)
     moved = lax.all_to_all(
         moved.reshape(PARTS, ROWS, LANES), "gy", split_axis=0, concat_axis=0, tiled=True
     )

time: 55.8 us -> 49.8 us (0.89)
  blocking collectives: 36.3 us -> 26.8 us
  starting transfers between devices: 7.59 us -> 10.9 us
  waiting for transfers between devices: 0.43 us -> 2.06 us
  Pallas kernels: 8.22 us -> 6.83 us
    all_to_all x1, blocking collectives: 24.7 us -> 16.1 us  [on_device(): lax.all_to_all(send, 'gy', split_axis=0, concat_axis=0, tiled=True, axis_...]
    ppermute x0 -> x1, starting transfers between devices: none -> 3.3 us  [on_device(): other = lax.ppermute(mine, 'gy', [(i, i ^ 1) for i in range(PARTS)])]
    ppermute x0 -> x1, waiting for transfers between devices: none -> 1.63 us  [on_device(): other = lax.ppermute(mine, 'gy', [(i, i ^ 1) for i in range(PARTS)])]
    pallas_call x1, Pallas kernels: 7.44 us -> 6.08 us  [on_device(): pl.pallas_call(advance_kernel, out_shape=f32(PARTS * ROWS, LANES), in_spe...]
    all_to_all x1, blocking collectives: 11.6 us -> 10.6 us  [on_device(): lax.all_to_all(moved.reshape(PARTS, ROWS, LANES), 'gy', split_axis=0, con...]
  transfers between devices with their start and end apart: 2 -> 3, of which waited for: 2 -> 3; matrix products, arithmetic and copies ran while one was open for 0% -> 0% of each run, Pallas kernels for 0% -> 0%
where the time goes in v2:
time: 49.8 us; the launch traced here: 49.5 us
  blocking collectives  26.8 us (54%)
  starting transfers between devices  10.9 us (22%)
  Pallas kernels  6.83 us (14%)
  waiting for transfers between devices  2.06 us (4%)
  other arithmetic  1.52 us (3%)
  local copies, waits for them, and re-layouts  0.81 us (2%)
  between operations  0.66 us (1%)
    all_to_all x1, blocking collectives, on_device(): lax.all_to_all(send, 'gy', split_axis=0, concat_axis=0, tiled=True, axis_...  16.1 us
    all_to_all x1, blocking collectives, on_device(): lax.all_to_all(moved.reshape(PARTS, ROWS, LANES), 'gy', split_axis=0, con...  10.6 us
    pallas_call x1, Pallas kernels, on_device(): pl.pallas_call(advance_kernel, out_shape=f32(PARTS * ROWS, LANES), in_spe...  6.08 us
    ppermute x1, starting transfers between devices, on_device(): up = lax.ppermute(up, 'gx', [((i + 1) % count, i) for i in range(count)])  5.05 us
    ppermute x1, starting transfers between devices, on_device(): other = lax.ppermute(mine, 'gy', [(i, i ^ 1) for i in range(PARTS)])  3.3 us
    ppermute x1, starting transfers between devices, on_device(): low = lax.ppermute(low, 'gx', [(i, (i + 1) % count) for i in range(count)])  2.54 us
    ppermute x1, waiting for transfers between devices, on_device(): other = lax.ppermute(mine, 'gy', [(i, i ^ 1) for i in range(PARTS)])  1.63 us
  transfers between devices with their start and end apart: 3, of which 3 were waited for; matrix products, arithmetic and copies ran while one was open for 0% of the time, Pallas kernels for 0%

profile of v2, /device:TPU:1, one launch (start us, length us, event | category | flops | bytes accessed | tf_op | source)
XLA Modules:
  0.0 49.5 jit_solution(17925766411386986455)
XLA Ops:
  0.6 0.7 %convert_bitcast_fusion = f32[1,16,128]{2,1,0:T(8,128)S(1)} fusion(s32[2,16]{1,0:T(2,128)} %param.8), kind=kLoop, calls=%fused_computation.1 | loop fusion | flops 2048 | bytes 8320 | tf_op jit(solution)/shard_map/broadcast_in_dim | solution.py:411
  1.3 0.8 %pad_maximum_fusion.held = f32[15,16,128]{2,1,0:T(8,128)S(1)} fusion(f32[1,16,128]{2,1,0:T(8,128)S(1)} %convert_bitcast_fusion, f32[6,16,128]{2,1,0:T(8,128)} %bitcast.13, f32[6,16,128]{2,1,0:T(8,128)} %bitcast.14, f32[2,16,128]{2,1,0:T(8,128)} %param.5), kind=kLoop, calls=%fused_computation | loop fusion | flops 92160 | bytes 245760 | tf_op jit(solution)/shard_map/concatenate | solution.py:410
  2.2 2.5 %collective-permute-start = (f32[72,128]{1,0:T(8,128)S(1)}, f32[72,128]{1,0:T(8,128)S(1)}, u32[]{:S(2)}, u32[]{:S(2)}) collective-permute-start(f32[72,128]{1,0:T(8,128)S(1)} %get-tuple-element.10), channel_id=1, source_target_pairs={{0,16},{16,32},{32,48},{48,64},{64,80},{80,96},{96,112},{112,128},... | collective-permute-start | bytes 110600 | tf_op jit(solution)/shard_map/ppermute | solution.py:421
  4.7 0.0 copy-start
  4.7 5.1 %collective-permute-start.1 = (f32[64,128]{1,0:T(8,128)S(1)}, f32[64,128]{1,0:T(8,128)S(1)}, u32[]{:S(2)}, u32[]{:S(2)}) collective-permute-start(f32[64,128]{1,0:T(8,128)S(1)} %get-tuple-element.11), channel_id=1, source_target_pairs={{16,0},{32,16},{48,32},{64,48},{80,64},{96,80},{112,96},{128,112},... | collective-permute-start | bytes 98312 | tf_op jit(solution)/shard_map/ppermute | solution.py:422
  9.8 0.0 copy-done
  9.8 0.1 reshape.26
  9.9 0.0 copy-start.1
  9.9 0.7 %copy-done.1 = s32[2]{0:T(128)S(1)} copy-done((s32[2]{0:T(128)S(1)}, s32[2]{0:T(128)}, u32[]{:S(2)}) %copy-start.1) | copy-done | bytes 32
  10.5 0.1 concatenate.7.scalars
  10.6 0.2 collective-permute-done.1.up
  10.8 0.2 collective-permute-done.low
  11.0 0.1 shard_map.77
  11.1 16.1 %all_to_all.10 = f32[8,144,128]{2,1,0:T(8,128)S(1)} all-to-all(f32[8,144,128]{2,1,0:T(8,128)S(1)} %get-tuple-element.16), channel_id=1, replica_groups={{0,2,4,6,8,10,12,14},{1,3,5,7,9,11,13,15},{16,18,20,22,24,26,28,30},{17..., dimensions={0} | all-to-all | bytes 1179648 | tf_op jit(solution)/shard_map/all_to_all | solution.py:437
  27.2 3.3 %collective-permute-start.2 = (f32[1152,128]{1,0:T(8,128)S(1)}, f32[1152,128]{1,0:T(8,128)S(1)}, u32[]{:S(2)}, u32[]{:S(2)}) collective-permute-start(f32[1152,128]{1,0:T(8,128)S(1)} %bitcast.9), channel_id=1, source_target_pairs={{0,1},{1,0},{2,3},{3,2},{4,5},{5,4},{6,7},{7,6},{8,9},{9,8},{10,11... | collective-permute-start | bytes 1769480 | tf_op jit(solution)/shard_map/ppermute | solution.py:441
  30.5 1.6 %collective-permute-done.2.other = f32[1152,128]{1,0:T(8,128)S(1)} collective-permute-done((f32[1152,128]{1,0:T(8,128)S(1)}, f32[1152,128]{1,0:T(8,128)S(1)}, u32[]{:S(2)}, u32[]{:S(2)}) %collective-permute-start.2) | collective-permute-done | bytes 589856 | tf_op jit(solution)/shard_map/ppermute | solution.py:441
  32.1 6.1 %shard_map.78 = f32[256,128]{1,0:T(8,128)S(1)} custom-call(s32[37]{0:T(128)S(1)} %concatenate.7.scalars, s32[4,128]{1,0:T(4,128)S(1)} %get-tuple-element.15.ghost_offsets, f32[1152,128]{1,0:T(8,128)S(1)} %bitcast.10, f32[1152,128]{1,0:T(8,128)S(1)} %collective-permute-done.2.other), custom_call_target="tpu_custom_call" | custom-call | tf_op jit(solution)/shard_map/pallas_call | solution.py:442
  38.2 10.6 %all_to_all.11 = f32[16,16,128]{2,1,0:T(8,128)S(1)} all-to-all(f32[16,16,128]{2,1,0:T(8,128)S(1)} %bitcast.11), channel_id=1, replica_groups=mesh['gx'=16,'gy'=16] {'gy'}, dimensions={0} | all-to-all | bytes 262144 | tf_op jit(solution)/shard_map/all_to_all | solution.py:450
  48.9 0.7 %shard_map.79 = (f32[2,16,128]{2,1,0:T(8,128)}, f32[3,2,16,128]{3,2,1,0:T(8,128)}, f32[3,2,16,128]{3,2,1,0:T(8,128)}) custom-call(f32[256,128]{1,0:T(8,128)S(1)} %bitcast.12), custom_call_target="tpu_custom_call" | custom-call | tf_op jit(solution)/shard_map/pallas_call | solution.py:453
  (1 shorter events, 0.0 us)
Async XLA Ops:
  2.2 8.8 %collective-permute-start = (f32[72,128]{1,0:T(8,128)S(1)}, f32[72,128]{1,0:T(8,128)S(1)}, u32[]{:S(2)}, u32[]{:S(2)}) collective-permute-start(f32[72,128]{1,0:T(8,128)S(1)} %get-tuple-element.10), channel_id=1, source_target_pairs={{0,16},{16,32},{32,48},{48,64},{64,80},{80,96},{96,112},{112,128},... | collective-permute-start | bytes 110600 | tf_op jit(solution)/shard_map/ppermute | solution.py:421
  4.7 5.1 %copy-start = (s32[2,16]{1,0:T(2,128)S(1)}, s32[2,16]{1,0:T(2,128)}, u32[]{:S(2)}) copy-start(s32[2,16]{1,0:T(2,128)} %param.8) | copy-start | bytes 388
  4.7 6.1 %collective-permute-start.1 = (f32[64,128]{1,0:T(8,128)S(1)}, f32[64,128]{1,0:T(8,128)S(1)}, u32[]{:S(2)}, u32[]{:S(2)}) collective-permute-start(f32[64,128]{1,0:T(8,128)S(1)} %get-tuple-element.11), channel_id=1, source_target_pairs={{16,0},{32,16},{48,32},{64,48},{80,64},{96,80},{112,96},{128,112},... | collective-permute-start | bytes 98312 | tf_op jit(solution)/shard_map/ppermute | solution.py:422
  9.9 0.7 %copy-start.1 = (s32[2]{0:T(128)S(1)}, s32[2]{0:T(128)}, u32[]{:S(2)}) copy-start(s32[2]{0:T(128)} %param.9) | copy-start | bytes 28
  27.2 4.9 %collective-permute-start.2 = (f32[1152,128]{1,0:T(8,128)S(1)}, f32[1152,128]{1,0:T(8,128)S(1)}, u32[]{:S(2)}, u32[]{:S(2)}) collective-permute-start(f32[1152,128]{1,0:T(8,128)S(1)} %bitcast.9), channel_id=1, source_target_pairs={{0,1},{1,0},{2,3},{3,2},{4,5},{5,4},{6,7},{7,6},{8,9},{9,8},{10,11... | collective-permute-start | bytes 1769480 | tf_op jit(solution)/shard_map/ppermute | solution.py:441

commit v3 on v2

--- a/solution.py
+++ b/solution.py
@@ -25,14 +25,16 @@
 CHUNK = 144
 
 
-def strip_kernel(held, low, up):
+def strip_kernel(held, offsets, low, up):
     for index in range(SLABS):
         rows = held[index]
         low[pl.ds(index, BELOW, stride=SLABS), :] = rows[ROWS - BELOW :]
         up[pl.ds(index, ABOVE, stride=SLABS), :] = rows[:ABOVE]
-    low[70:72, :] = held[SLABS, 0:2, :]
-    up[56:58, :] = held[SLABS, 0:2, :]
-    up[58:64, :] = jnp.zeros((6, LANES), jnp.float32)
+    shifts = offsets[...].astype(jnp.float32)
+    low[70:72, :] = jnp.zeros((2, LANES), jnp.float32)
+    up[56:64, :] = jnp.zeros((8, LANES), jnp.float32)
+    low[70:72, 0:ROWS] = shifts
+    up[56:58, 0:ROWS] = shifts
 
 
 def pack_kernel(held, low, up, send, ghost_offsets, rows_of):
@@ -256,18 +258,6 @@
         update(row, row == 1)
 
 
-def rolled(twice, amount, lane):
-    blocks = amount // LANES
-    cells = amount % LANES
-    parts = []
-    for odd in range(2):
-        start = PARTS - blocks + odd
-        here = pltpu.roll(twice[pl.ds(start, HALF, stride=2), :], cells, 1)
-        before = pltpu.roll(twice[pl.ds(start - 1, HALF, stride=2), :], cells, 1)
-        parts.append(jnp.where(lane >= cells, here, before))
-    return jnp.stack(parts)
-
-
 def to_blocks(ref, start, stride, values):
     for odd in range(2):
         ref[pl.ds(start + odd * stride, HALF, stride=2 * stride), :] = values[odd]
@@ -311,13 +301,21 @@
     lax.fori_loop(1, FULL + 1, fetch, 0)
 
     def turn(ref, row, amount, members=range(7)):
+        blocks = amount // LANES
+        cells = amount % LANES
+        swap = blocks % 2
+        here = lane >= cells
         slabs = [(member, z) for member in members for z in range(2)]
         for place, (member, z) in enumerate(slabs):
-            values = ref[row, member, z]
-            to_blocks(twice.at[place], 0, 1, values)
-            to_blocks(twice.at[place], PARTS, 1, values)
+            for parity, values in ((0, ref[row, member, z, swap]), (1, ref[row, member, z, 1 - swap])):
+                twice[place, parity, 0:HALF, :] = values
+                twice[place, parity, HALF : 2 * HALF, :] = values
         for place, (member, z) in enumerate(slabs):
-            ref[row, member, z] = rolled(twice.at[place], amount, lane)
+            even = twice[place, 0, pl.ds((2 * HALF - blocks) // 2, HALF), :]
+            odd = twice[place, 1, pl.ds(HALF - blocks // 2, HALF), :]
+            even, odd = pltpu.roll(even, cells, 1), pltpu.roll(odd, cells, 1)
+            ref[row, member, z, 0] = jnp.where(here, even, pltpu.roll(odd, 1, 0))
+            ref[row, member, z, 1] = jnp.where(here, odd, even)
 
     def ghosts(row, carry):
         place_of = row_of - BELOW + row
@@ -400,23 +398,20 @@
         pltpu.VMEM((FULL + 1, 7) + row, jnp.float32),
         pltpu.VMEM((FULL + 1, FLUXES, 2, HALF, LANES), jnp.float32),
         pltpu.VMEM((FULL + 1, 2) + row, jnp.float32),
-        pltpu.VMEM((SLABS, 2 * ROWS, LANES), jnp.float32),
+        pltpu.VMEM((SLABS, 2, 2 * HALF, LANES), jnp.float32),
     ]
 
 
 def on_device(density, momentum, field, fargo_offsets, shear_shift):
-    shifts = jnp.pad(fargo_offsets, ((0, ROWS - LEVELS), (0, LANES - ROWS))).astype(jnp.float32)
     block = (-1, ROWS, LANES)
-    held = jnp.concatenate(
-        [density, momentum.reshape(block), field.reshape(block), shifts[None]], axis=0
-    )
+    held = jnp.concatenate([density, momentum.reshape(block), field.reshape(block)], axis=0)
     low, up = pl.pallas_call(
         strip_kernel,
         out_shape=(f32(LOW_ROWS, LANES), f32(UP_ROWS, LANES)),
-        in_specs=in_vmem(1),
+        in_specs=in_vmem(2),
         out_specs=tuple(in_vmem(2)),
         compiler_params=params,
-    )(held)
+    )(held, fargo_offsets)
     count = lax.axis_size("gx")
     low = lax.ppermute(low, "gx", [(i, (i + 1) % count) for i in range(count)])
     up = lax.ppermute(up, "gx", [((i + 1) % count, i) for i in range(count)])

time: 49.8 us -> 49 us (0.984)
  other arithmetic: 1.52 us -> 0.84 us
    broadcast_in_dim x1 -> x0, other arithmetic: 0.69 us -> none  [on_device(): shifts[None]]
where the time goes in v3:
time: 49 us; the launch traced here: 48.8 us
  blocking collectives  26.8 us (55%)
  starting transfers between devices  10.9 us (22%)
  Pallas kernels  6.73 us (14%)
  waiting for transfers between devices  2.08 us (4%)
  other arithmetic  0.84 us (2%)
  local copies, waits for them, and re-layouts  0.81 us (2%)
  between operations  0.67 us (1%)
    all_to_all x1, blocking collectives, on_device(): lax.all_to_all(send, 'gy', split_axis=0, concat_axis=0, tiled=True, axis_...  16.1 us
    all_to_all x1, blocking collectives, on_device(): lax.all_to_all(moved.reshape(PARTS, ROWS, LANES), 'gy', split_axis=0, con...  10.6 us
    pallas_call x1, Pallas kernels, on_device(): pl.pallas_call(advance_kernel, out_shape=f32(PARTS * ROWS, LANES), in_spe...  5.98 us
    ppermute x1, starting transfers between devices, on_device(): up = lax.ppermute(up, 'gx', [((i + 1) % count, i) for i in range(count)])  5.04 us
    ppermute x1, starting transfers between devices, on_device(): other = lax.ppermute(mine, 'gy', [(i, i ^ 1) for i in range(PARTS)])  3.3 us
    ppermute x1, starting transfers between devices, on_device(): low = lax.ppermute(low, 'gx', [(i, (i + 1) % count) for i in range(count)])  2.54 us
    ppermute x1, waiting for transfers between devices, on_device(): other = lax.ppermute(mine, 'gy', [(i, i ^ 1) for i in range(PARTS)])  1.63 us
  transfers between devices with their start and end apart: 3, of which 3 were waited for; matrix products, arithmetic and copies ran while one was open for 0% of the time, Pallas kernels for 0%

profile of v3, /device:TPU:1, one launch (start us, length us, event | category | flops | bytes accessed | tf_op | source)
XLA Modules:
  0.0 48.8 jit_solution(14761548620380690777)
XLA Ops:
  0.6 0.0 copy-start
  0.6 0.8 %pad_maximum_fusion.held = f32[14,16,128]{2,1,0:T(8,128)S(1)} fusion(f32[6,16,128]{2,1,0:T(8,128)} %bitcast.11, f32[6,16,128]{2,1,0:T(8,128)} %bitcast.12, f32[2,16,128]{2,1,0:T(8,128)} %param.5), kind=kLoop, calls=%fused_computation | loop fusion | flops 57344 | bytes 229376 | tf_op jit(solution)/shard_map/concatenate | solution.py:407
  1.5 0.0 copy-done
  1.5 2.5 %collective-permute-start = (f32[72,128]{1,0:T(8,128)S(1)}, f32[72,128]{1,0:T(8,128)S(1)}, u32[]{:S(2)}, u32[]{:S(2)}) collective-permute-start(f32[72,128]{1,0:T(8,128)S(1)} %get-tuple-element.10), channel_id=1, source_target_pairs={{0,16},{16,32},{32,48},{48,64},{64,80},{80,96},{96,112},{112,128},... | collective-permute-start | bytes 110600 | tf_op jit(solution)/shard_map/ppermute | solution.py:416
  4.0 5.0 %collective-permute-start.1 = (f32[64,128]{1,0:T(8,128)S(1)}, f32[64,128]{1,0:T(8,128)S(1)}, u32[]{:S(2)}, u32[]{:S(2)}) collective-permute-start(f32[64,128]{1,0:T(8,128)S(1)} %get-tuple-element.11), channel_id=1, source_target_pairs={{16,0},{32,16},{48,32},{64,48},{80,64},{96,80},{112,96},{128,112},... | collective-permute-start | bytes 98312 | tf_op jit(solution)/shard_map/ppermute | solution.py:417
  9.1 0.1 reshape.26
  9.2 0.0 copy-start.1
  9.2 0.7 %copy-done.1 = s32[2]{0:T(128)S(1)} copy-done((s32[2]{0:T(128)S(1)}, s32[2]{0:T(128)}, u32[]{:S(2)}) %copy-start.1) | copy-done | bytes 32
  9.8 0.1 concatenate.7.scalars
  9.9 0.2 collective-permute-done.1.up
  10.1 0.2 collective-permute-done.low
  10.3 0.1 shard_map.77
  10.4 16.1 %all_to_all.10 = f32[8,144,128]{2,1,0:T(8,128)S(1)} all-to-all(f32[8,144,128]{2,1,0:T(8,128)S(1)} %get-tuple-element.16), channel_id=1, replica_groups={{0,2,4,6,8,10,12,14},{1,3,5,7,9,11,13,15},{16,18,20,22,24,26,28,30},{17..., dimensions={0} | all-to-all | bytes 1179648 | tf_op jit(solution)/shard_map/all_to_all | solution.py:432
  26.5 3.3 %collective-permute-start.2 = (f32[1152,128]{1,0:T(8,128)S(1)}, f32[1152,128]{1,0:T(8,128)S(1)}, u32[]{:S(2)}, u32[]{:S(2)}) collective-permute-start(f32[1152,128]{1,0:T(8,128)S(1)} %bitcast.7), channel_id=1, source_target_pairs={{0,1},{1,0},{2,3},{3,2},{4,5},{5,4},{6,7},{7,6},{8,9},{9,8},{10,11... | collective-permute-start | bytes 1769480 | tf_op jit(solution)/shard_map/ppermute | solution.py:436
  29.8 1.6 %collective-permute-done.2.other = f32[1152,128]{1,0:T(8,128)S(1)} collective-permute-done((f32[1152,128]{1,0:T(8,128)S(1)}, f32[1152,128]{1,0:T(8,128)S(1)}, u32[]{:S(2)}, u32[]{:S(2)}) %collective-permute-start.2) | collective-permute-done | bytes 589856 | tf_op jit(solution)/shard_map/ppermute | solution.py:436
  31.5 6.0 %shard_map.78 = f32[256,128]{1,0:T(8,128)S(1)} custom-call(s32[37]{0:T(128)S(1)} %concatenate.7.scalars, s32[4,128]{1,0:T(4,128)S(1)} %get-tuple-element.15.ghost_offsets, f32[1152,128]{1,0:T(8,128)S(1)} %bitcast.8, f32[1152,128]{1,0:T(8,128)S(1)} %collective-permute-done.2.other), custom_call_target="tpu_custom_call" | custom-call | tf_op jit(solution)/shard_map/pallas_call | solution.py:437
  37.5 10.6 %all_to_all.11 = f32[16,16,128]{2,1,0:T(8,128)S(1)} all-to-all(f32[16,16,128]{2,1,0:T(8,128)S(1)} %bitcast.9), channel_id=1, replica_groups=mesh['gx'=16,'gy'=16] {'gy'}, dimensions={0} | all-to-all | bytes 262144 | tf_op jit(solution)/shard_map/all_to_all | solution.py:445
  48.1 0.7 %shard_map.79 = (f32[2,16,128]{2,1,0:T(8,128)}, f32[3,2,16,128]{3,2,1,0:T(8,128)}, f32[3,2,16,128]{3,2,1,0:T(8,128)}) custom-call(f32[256,128]{1,0:T(8,128)S(1)} %bitcast.10), custom_call_target="tpu_custom_call" | custom-call | tf_op jit(solution)/shard_map/pallas_call | solution.py:448
  (1 shorter events, 0.0 us)
Async XLA Ops:
  0.6 0.8 %copy-start = (s32[2,16]{1,0:T(2,128)S(1)}, s32[2,16]{1,0:T(2,128)}, u32[]{:S(2)}) copy-start(s32[2,16]{1,0:T(2,128)} %offsets.1) | copy-start | bytes 388
  1.5 8.8 %collective-permute-start = (f32[72,128]{1,0:T(8,128)S(1)}, f32[72,128]{1,0:T(8,128)S(1)}, u32[]{:S(2)}, u32[]{:S(2)}) collective-permute-start(f32[72,128]{1,0:T(8,128)S(1)} %get-tuple-element.10), channel_id=1, source_target_pairs={{0,16},{16,32},{32,48},{48,64},{64,80},{80,96},{96,112},{112,128},... | collective-permute-start | bytes 110600 | tf_op jit(solution)/shard_map/ppermute | solution.py:416
  4.0 6.1 %collective-permute-start.1 = (f32[64,128]{1,0:T(8,128)S(1)}, f32[64,128]{1,0:T(8,128)S(1)}, u32[]{:S(2)}, u32[]{:S(2)}) collective-permute-start(f32[64,128]{1,0:T(8,128)S(1)} %get-tuple-element.11), channel_id=1, source_target_pairs={{16,0},{32,16},{48,32},{64,48},{80,64},{96,80},{112,96},{128,112},... | collective-permute-start | bytes 98312 | tf_op jit(solution)/shard_map/ppermute | solution.py:417
  9.2 0.7 %copy-start.1 = (s32[2]{0:T(128)S(1)}, s32[2]{0:T(128)}, u32[]{:S(2)}) copy-start(s32[2]{0:T(128)} %param.9) | copy-start | bytes 28
  26.5 4.9 %collective-permute-start.2 = (f32[1152,128]{1,0:T(8,128)S(1)}, f32[1152,128]{1,0:T(8,128)S(1)}, u32[]{:S(2)}, u32[]{:S(2)}) collective-permute-start(f32[1152,128]{1,0:T(8,128)S(1)} %bitcast.7), channel_id=1, source_target_pairs={{0,1},{1,0},{2,3},{3,2},{4,5},{5,4},{6,7},{7,6},{8,9},{9,8},{10,11... | collective-permute-start | bytes 1769480 | tf_op jit(solution)/shard_map/ppermute | solution.py:436

commit v4 on v3

--- a/solution.py
+++ b/solution.py
@@ -50,6 +50,7 @@
         send[pair, 142:CHUNK, :] = jnp.zeros((CHUNK - 142, LANES), jnp.float32)
     ghost_offsets[0:2, :] = low[70:72, :].astype(jnp.int32)
     ghost_offsets[2:4, :] = up[56:58, :].astype(jnp.int32)
+    ghost_offsets[4:8, :] = jnp.zeros((4, LANES), jnp.int32)
 
 
 def y_ahead(values, lane):
@@ -264,8 +265,8 @@
 
 
 def advance_kernel(
-    scalars,
-    ghost_offsets,
+    scalars_of,
+    ghost_offsets_of,
     mine,
     other,
     send,
@@ -275,11 +276,20 @@
     fluxes,
     edges,
     twice,
+    scalars,
+    ghost_offsets,
+    arrived,
 ):
+    copies = [
+        pltpu.make_async_copy(scalars_of, scalars, arrived.at[0]),
+        pltpu.make_async_copy(ghost_offsets_of, ghost_offsets, arrived.at[1]),
+    ]
+    for copy in copies:
+        copy.start()
     cycle = PARTS * LANES
-    radial = scalars[0]
-    own = scalars[1]
-    radial_count = scalars[2]
+    radial = lax.axis_index("gx")
+    own = lax.axis_index("gy")
+    radial_count = lax.axis_size("gx")
     row_of = radial * ROWS + own
     total = radial_count * ROWS
     lane = lax.broadcasted_iota(jnp.int32, (HALF, LANES), 1)
@@ -317,7 +327,10 @@
             ref[row, member, z, 0] = jnp.where(here, even, pltpu.roll(odd, 1, 0))
             ref[row, member, z, 1] = jnp.where(here, odd, even)
 
-    def ghosts(row, carry):
+    for copy in copies:
+        copy.wait()
+
+    def ghosts(row, members):
         place_of = row_of - BELOW + row
         below = place_of < 0
         above = place_of >= total
@@ -325,11 +338,14 @@
         @pl.when(below | above)
         def _():
             shift = scalars[3]
-            turn(state, row, jnp.where(below, cycle - shift, shift) % cycle)
-
+            turn(state, row, jnp.where(below, cycle - shift, shift) % cycle, members)
+
+    def whole_ghosts(row, carry):
+        ghosts(row, range(7))
         return carry
 
-    lax.fori_loop(0, FULL + 1, ghosts, 0)
+    ghosts(0, range(4, 5))
+    lax.fori_loop(1, FULL + 1, whole_ghosts, 0)
 
     common = (prim, fluxes, edges, lane)
     stage(9, state, None, first, *common)
@@ -399,6 +415,9 @@
         pltpu.VMEM((FULL + 1, FLUXES, 2, HALF, LANES), jnp.float32),
         pltpu.VMEM((FULL + 1, 2) + row, jnp.float32),
         pltpu.VMEM((SLABS, 2, 2 * HALF, LANES), jnp.float32),
+        pltpu.SMEM((3 + LEVELS + LEVELS * ROWS,), jnp.int32),
+        pltpu.SMEM((8, LANES), jnp.int32),
+        pltpu.SemaphoreType.DMA((2,)),
     ]
 
 
@@ -422,7 +441,7 @@
     low, up, scalars = lax.optimization_barrier((low, up, scalars))
     send, ghost_offsets = pl.pallas_call(
         pack_kernel,
-        out_shape=(f32(HALF, CHUNK, LANES), jax.ShapeDtypeStruct((4, LANES), jnp.int32)),
+        out_shape=(f32(HALF, CHUNK, LANES), jax.ShapeDtypeStruct((8, LANES), jnp.int32)),
         in_specs=in_vmem(3),
         out_specs=tuple(in_vmem(2)),
         scratch_shapes=[pltpu.VMEM((352, LANES), jnp.float32)],
@@ -437,7 +456,7 @@
     moved = pl.pallas_call(
         advance_kernel,
         out_shape=f32(PARTS * ROWS, LANES),
-        in_specs=in_smem(2) + in_vmem(2),
+        in_specs=in_vmem(4),
         out_specs=in_vmem(1)[0],
         scratch_shapes=scratch(),
         compiler_params=params,

time: 49 us -> 48.6 us (level)
  no operation moved by 1% of the time
where the time goes in v4:
time: 48.6 us; the launch traced here: 48.4 us
  blocking collectives  26.8 us (55%)
  starting transfers between devices  10.9 us (22%)
  Pallas kernels  6.32 us (13%)
  waiting for transfers between devices  2.08 us (4%)
  other arithmetic  0.84 us (2%)
  local copies, waits for them, and re-layouts  0.81 us (2%)
  between operations  0.67 us (1%)
    all_to_all x1, blocking collectives, on_device(): lax.all_to_all(send, 'gy', split_axis=0, concat_axis=0, tiled=True, axis_...  16.1 us
    all_to_all x1, blocking collectives, on_device(): lax.all_to_all(moved.reshape(PARTS, ROWS, LANES), 'gy', split_axis=0, con...  10.6 us
    pallas_call x1, Pallas kernels, on_device(): pl.pallas_call(advance_kernel, out_shape=f32(PARTS * ROWS, LANES), in_spe...  5.58 us
    ppermute x1, starting transfers between devices, on_device(): up = lax.ppermute(up, 'gx', [((i + 1) % count, i) for i in range(count)])  5.04 us
    ppermute x1, starting transfers between devices, on_device(): other = lax.ppermute(mine, 'gy', [(i, i ^ 1) for i in range(PARTS)])  3.3 us
    ppermute x1, starting transfers between devices, on_device(): low = lax.ppermute(low, 'gx', [(i, (i + 1) % count) for i in range(count)])  2.54 us
    ppermute x1, waiting for transfers between devices, on_device(): other = lax.ppermute(mine, 'gy', [(i, i ^ 1) for i in range(PARTS)])  1.63 us
  transfers between devices with their start and end apart: 3, of which 3 were waited for; matrix products, arithmetic and copies ran while one was open for 0% of the time, Pallas kernels for 0%

profile of v4, /device:TPU:1, one launch (start us, length us, event | category | flops | bytes accessed | tf_op | source)
XLA Modules:
  0.0 48.4 jit_solution(11060638587239657770)
XLA Ops:
  0.6 0.0 copy-start
  0.6 0.8 %pad_maximum_fusion.held = f32[14,16,128]{2,1,0:T(8,128)S(1)} fusion(f32[6,16,128]{2,1,0:T(8,128)} %bitcast.11, f32[6,16,128]{2,1,0:T(8,128)} %bitcast.12, f32[2,16,128]{2,1,0:T(8,128)} %param.5), kind=kLoop, calls=%fused_computation | loop fusion | flops 57344 | bytes 229376 | tf_op jit(solution)/shard_map/concatenate | solution.py:426
  1.5 0.0 copy-done
  1.5 2.5 %collective-permute-start = (f32[72,128]{1,0:T(8,128)S(1)}, f32[72,128]{1,0:T(8,128)S(1)}, u32[]{:S(2)}, u32[]{:S(2)}) collective-permute-start(f32[72,128]{1,0:T(8,128)S(1)} %get-tuple-element.10), channel_id=1, source_target_pairs={{0,16},{16,32},{32,48},{48,64},{64,80},{80,96},{96,112},{112,128},... | collective-permute-start | bytes 110600 | tf_op jit(solution)/shard_map/ppermute | solution.py:435
  4.0 5.0 %collective-permute-start.1 = (f32[64,128]{1,0:T(8,128)S(1)}, f32[64,128]{1,0:T(8,128)S(1)}, u32[]{:S(2)}, u32[]{:S(2)}) collective-permute-start(f32[64,128]{1,0:T(8,128)S(1)} %get-tuple-element.11), channel_id=1, source_target_pairs={{16,0},{32,16},{48,32},{64,48},{80,64},{96,80},{112,96},{128,112},... | collective-permute-start | bytes 98312 | tf_op jit(solution)/shard_map/ppermute | solution.py:436
  9.1 0.1 reshape.26
  9.2 0.0 copy-start.1
  9.2 0.7 %copy-done.1 = s32[2]{0:T(128)S(1)} copy-done((s32[2]{0:T(128)S(1)}, s32[2]{0:T(128)}, u32[]{:S(2)}) %copy-start.1) | copy-done | bytes 32
  9.8 0.1 concatenate.7.scalars_of
  9.9 0.2 collective-permute-done.1.up
  10.1 0.2 collective-permute-done.low
  10.3 0.1 shard_map.77
  10.4 16.1 %all_to_all.10 = f32[8,144,128]{2,1,0:T(8,128)S(1)} all-to-all(f32[8,144,128]{2,1,0:T(8,128)S(1)} %get-tuple-element.16), channel_id=1, replica_groups={{0,2,4,6,8,10,12,14},{1,3,5,7,9,11,13,15},{16,18,20,22,24,26,28,30},{17..., dimensions={0} | all-to-all | bytes 1179648 | tf_op jit(solution)/shard_map/all_to_all | solution.py:451
  26.5 3.3 %collective-permute-start.2 = (f32[1152,128]{1,0:T(8,128)S(1)}, f32[1152,128]{1,0:T(8,128)S(1)}, u32[]{:S(2)}, u32[]{:S(2)}) collective-permute-start(f32[1152,128]{1,0:T(8,128)S(1)} %bitcast.7), channel_id=1, source_target_pairs={{0,1},{1,0},{2,3},{3,2},{4,5},{5,4},{6,7},{7,6},{8,9},{9,8},{10,11... | collective-permute-start | bytes 1769480 | tf_op jit(solution)/shard_map/ppermute | solution.py:455
  29.8 1.6 %collective-permute-done.2.other = f32[1152,128]{1,0:T(8,128)S(1)} collective-permute-done((f32[1152,128]{1,0:T(8,128)S(1)}, f32[1152,128]{1,0:T(8,128)S(1)}, u32[]{:S(2)}, u32[]{:S(2)}) %collective-permute-start.2) | collective-permute-done | bytes 589856 | tf_op jit(solution)/shard_map/ppermute | solution.py:455
  31.5 5.6 %shard_map.78 = f32[256,128]{1,0:T(8,128)S(1)} custom-call(s32[37]{0:T(128)S(1)} %concatenate.7.scalars_of, s32[8,128]{1,0:T(8,128)S(1)} %get-tuple-element.15.ghost_offsets_of, f32[1152,128]{1,0:T(8,128)S(1)} %bitcast.8, f32[1152,128]{1,0:T(8,128)S(1)} %collective-permute-done.2.other), custom_call_target="tpu_custom_call" | custom-call | tf_op jit(solution)/shard_map/pallas_call | solution.py:456
  37.1 10.6 %all_to_all.11 = f32[16,16,128]{2,1,0:T(8,128)S(1)} all-to-all(f32[16,16,128]{2,1,0:T(8,128)S(1)} %bitcast.9), channel_id=1, replica_groups=mesh['gx'=16,'gy'=16] {'gy'}, dimensions={0} | all-to-all | bytes 262144 | tf_op jit(solution)/shard_map/all_to_all | solution.py:464
  47.7 0.7 %shard_map.79 = (f32[2,16,128]{2,1,0:T(8,128)}, f32[3,2,16,128]{3,2,1,0:T(8,128)}, f32[3,2,16,128]{3,2,1,0:T(8,128)}) custom-call(f32[256,128]{1,0:T(8,128)S(1)} %bitcast.10), custom_call_target="tpu_custom_call" | custom-call | tf_op jit(solution)/shard_map/pallas_call | solution.py:467
  (1 shorter events, 0.0 us)
Async XLA Ops:
  0.6 0.8 %copy-start = (s32[2,16]{1,0:T(2,128)S(1)}, s32[2,16]{1,0:T(2,128)}, u32[]{:S(2)}) copy-start(s32[2,16]{1,0:T(2,128)} %offsets.1) | copy-start | bytes 388
  1.5 8.8 %collective-permute-start = (f32[72,128]{1,0:T(8,128)S(1)}, f32[72,128]{1,0:T(8,128)S(1)}, u32[]{:S(2)}, u32[]{:S(2)}) collective-permute-start(f32[72,128]{1,0:T(8,128)S(1)} %get-tuple-element.10), channel_id=1, source_target_pairs={{0,16},{16,32},{32,48},{48,64},{64,80},{80,96},{96,112},{112,128},... | collective-permute-start | bytes 110600 | tf_op jit(solution)/shard_map/ppermute | solution.py:435
  4.0 6.1 %collective-permute-start.1 = (f32[64,128]{1,0:T(8,128)S(1)}, f32[64,128]{1,0:T(8,128)S(1)}, u32[]{:S(2)}, u32[]{:S(2)}) collective-permute-start(f32[64,128]{1,0:T(8,128)S(1)} %get-tuple-element.11), channel_id=1, source_target_pairs={{16,0},{32,16},{48,32},{64,48},{80,64},{96,80},{112,96},{128,112},... | collective-permute-start | bytes 98312 | tf_op jit(solution)/shard_map/ppermute | solution.py:436
  9.2 0.7 %copy-start.1 = (s32[2]{0:T(128)S(1)}, s32[2]{0:T(128)}, u32[]{:S(2)}) copy-start(s32[2]{0:T(128)} %param.9) | copy-start | bytes 28
  26.5 4.9 %collective-permute-start.2 = (f32[1152,128]{1,0:T(8,128)S(1)}, f32[1152,128]{1,0:T(8,128)S(1)}, u32[]{:S(2)}, u32[]{:S(2)}) collective-permute-start(f32[1152,128]{1,0:T(8,128)S(1)} %bitcast.7), channel_id=1, source_target_pairs={{0,1},{1,0},{2,3},{3,2},{4,5},{5,4},{6,7},{7,6},{8,9},{9,8},{10,11... | collective-permute-start | bytes 1769480 | tf_op jit(solution)/shard_map/ppermute | solution.py:455

commit v5 on v4

--- a/solution.py
+++ b/solution.py
@@ -310,42 +310,49 @@
 
     lax.fori_loop(1, FULL + 1, fetch, 0)
 
-    def turn(ref, row, amount, members=range(7)):
-        blocks = amount // LANES
-        cells = amount % LANES
-        swap = blocks % 2
-        here = lane >= cells
-        slabs = [(member, z) for member in members for z in range(2)]
-        for place, (member, z) in enumerate(slabs):
+    def turn(ref, turns):
+        slabs = []
+        for row, amount, members in turns:
+            blocks = amount // LANES
+            slabs += [(row, blocks, amount % LANES, m, z) for m in members for z in range(2)]
+        for place, (row, blocks, cells, member, z) in enumerate(slabs):
+            swap = blocks % 2
             for parity, values in ((0, ref[row, member, z, swap]), (1, ref[row, member, z, 1 - swap])):
                 twice[place, parity, 0:HALF, :] = values
                 twice[place, parity, HALF : 2 * HALF, :] = values
-        for place, (member, z) in enumerate(slabs):
+        for place, (row, blocks, cells, member, z) in enumerate(slabs):
+            here = lane >= cells
             even = twice[place, 0, pl.ds((2 * HALF - blocks) // 2, HALF), :]
             odd = twice[place, 1, pl.ds(HALF - blocks // 2, HALF), :]
             even, odd = pltpu.roll(even, cells, 1), pltpu.roll(odd, cells, 1)
             ref[row, member, z, 0] = jnp.where(here, even, pltpu.roll(odd, 1, 0))
             ref[row, member, z, 1] = jnp.where(here, odd, even)
 
+    whole, radial_only = range(7), range(4, 5)
     for copy in copies:
         copy.wait()
-
-    def ghosts(row, members):
-        place_of = row_of - BELOW + row
-        below = place_of < 0
-        above = place_of >= total
-
-        @pl.when(below | above)
-        def _():
-            shift = scalars[3]
-            turn(state, row, jnp.where(below, cycle - shift, shift) % cycle, members)
-
-    def whole_ghosts(row, carry):
-        ghosts(row, range(7))
-        return carry
-
-    ghosts(0, range(4, 5))
-    lax.fori_loop(1, FULL + 1, whole_ghosts, 0)
+    shift = scalars[3]
+
+    @pl.when(row_of < BELOW)
+    def _():
+        back = (cycle - shift) % cycle
+        turn(
+            state,
+            [
+                (row, jnp.where(row_of - BELOW + row < 0, back, 0), radial_only if row == 0 else whole)
+                for row in range(BELOW)
+            ],
+        )
+
+    @pl.when(row_of + ABOVE >= total)
+    def _():
+        turn(
+            state,
+            [
+                (row, jnp.where(row_of - BELOW + row >= total, shift % cycle, 0), whole)
+                for row in range(BELOW + 1, FULL + 1)
+            ],
+        )
 
     common = (prim, fluxes, edges, lane)
     stage(9, state, None, first, *common)
@@ -364,15 +371,14 @@
         amount = offset + jnp.where(
             place_of < 0, -change, jnp.where(place_of >= total, change, 0)
         )
-        turn(state, row, (amount + 2 * cycle) % cycle, range(4, 5) if row == 0 else range(7))
-
-    for row in range(6):
-        remap(row)
+        return row, (amount + 2 * cycle) % cycle, radial_only if row == 0 else whole
+
+    turn(state, [remap(row) for row in range(6)])
 
     stage(5, state, None, first, *common)
     stage(3, first, state, state, *common)
 
-    turn(state, 1, scalars[5 + ROWS + own] % cycle)
+    turn(state, [(1, scalars[5 + ROWS + own] % cycle, whole)])
     for index in range(SLABS):
         to_blocks(send, index, ROWS, state[1, index // 2, index % 2])
     for index in range(SLABS, ROWS):
@@ -414,7 +420,7 @@
         pltpu.VMEM((FULL + 1, 7) + row, jnp.float32),
         pltpu.VMEM((FULL + 1, FLUXES, 2, HALF, LANES), jnp.float32),
         pltpu.VMEM((FULL + 1, 2) + row, jnp.float32),
-        pltpu.VMEM((SLABS, 2, 2 * HALF, LANES), jnp.float32),
+        pltpu.VMEM((72, 2, 2 * HALF, LANES), jnp.float32),
         pltpu.SMEM((3 + LEVELS + LEVELS * ROWS,), jnp.int32),
         pltpu.SMEM((8, LANES), jnp.int32),
         pltpu.SemaphoreType.DMA((2,)),

time: 48.6 us -> 48.3 us (level)
  no operation moved by 1% of the time
where the time goes in v5:
time: 48.3 us; the launch traced here: 48.1 us
  blocking collectives  26.6 us (55%)
  starting transfers between devices  10.9 us (23%)
  Pallas kernels  6.15 us (13%)
  waiting for transfers between devices  2.08 us (4%)
  other arithmetic  0.84 us (2%)
  local copies, waits for them, and re-layouts  0.81 us (2%)
  between operations  0.67 us (1%)
    all_to_all x1, blocking collectives, on_device(): lax.all_to_all(send, 'gy', split_axis=0, concat_axis=0, tiled=True, axis_...  16.1 us
    all_to_all x1, blocking collectives, on_device(): lax.all_to_all(moved.reshape(PARTS, ROWS, LANES), 'gy', split_axis=0, con...  10.5 us
    pallas_call x1, Pallas kernels, on_device(): pl.pallas_call(advance_kernel, out_shape=f32(PARTS * ROWS, LANES), in_spe...  5.4 us
    ppermute x1, starting transfers between devices, on_device(): up = lax.ppermute(up, 'gx', [((i + 1) % count, i) for i in range(count)])  5.04 us
    ppermute x1, starting transfers between devices, on_device(): other = lax.ppermute(mine, 'gy', [(i, i ^ 1) for i in range(PARTS)])  3.3 us
    ppermute x1, starting transfers between devices, on_device(): low = lax.ppermute(low, 'gx', [(i, (i + 1) % count) for i in range(count)])  2.54 us
    ppermute x1, waiting for transfers between devices, on_device(): other = lax.ppermute(mine, 'gy', [(i, i ^ 1) for i in range(PARTS)])  1.63 us
  transfers between devices with their start and end apart: 3, of which 3 were waited for; matrix products, arithmetic and copies ran while one was open for 0% of the time, Pallas kernels for 0%

profile of v5, /device:TPU:1, one launch (start us, length us, event | category | flops | bytes accessed | tf_op | source)
XLA Modules:
  0.0 48.1 jit_solution(8987300304270210615)
XLA Ops:
  0.6 0.0 copy-start
  0.6 0.8 %pad_maximum_fusion.held = f32[14,16,128]{2,1,0:T(8,128)S(1)} fusion(f32[6,16,128]{2,1,0:T(8,128)} %bitcast.11, f32[6,16,128]{2,1,0:T(8,128)} %bitcast.12, f32[2,16,128]{2,1,0:T(8,128)} %param.5), kind=kLoop, calls=%fused_computation | loop fusion | flops 57344 | bytes 229376 | tf_op jit(solution)/shard_map/concatenate | solution.py:432
  1.5 0.0 copy-done
  1.5 2.5 %collective-permute-start = (f32[72,128]{1,0:T(8,128)S(1)}, f32[72,128]{1,0:T(8,128)S(1)}, u32[]{:S(2)}, u32[]{:S(2)}) collective-permute-start(f32[72,128]{1,0:T(8,128)S(1)} %get-tuple-element.10), channel_id=1, source_target_pairs={{0,16},{16,32},{32,48},{48,64},{64,80},{80,96},{96,112},{112,128},... | collective-permute-start | bytes 110600 | tf_op jit(solution)/shard_map/ppermute | solution.py:441
  4.0 5.0 %collective-permute-start.1 = (f32[64,128]{1,0:T(8,128)S(1)}, f32[64,128]{1,0:T(8,128)S(1)}, u32[]{:S(2)}, u32[]{:S(2)}) collective-permute-start(f32[64,128]{1,0:T(8,128)S(1)} %get-tuple-element.11), channel_id=1, source_target_pairs={{16,0},{32,16},{48,32},{64,48},{80,64},{96,80},{112,96},{128,112},... | collective-permute-start | bytes 98312 | tf_op jit(solution)/shard_map/ppermute | solution.py:442
  9.1 0.1 reshape.26
  9.2 0.0 copy-start.1
  9.2 0.7 %copy-done.1 = s32[2]{0:T(128)S(1)} copy-done((s32[2]{0:T(128)S(1)}, s32[2]{0:T(128)}, u32[]{:S(2)}) %copy-start.1) | copy-done | bytes 32
  9.8 0.1 concatenate.7.scalars_of
  9.9 0.2 collective-permute-done.1.up
  10.1 0.2 collective-permute-done.low
  10.3 0.1 shard_map.77
  10.4 16.1 %all_to_all.10 = f32[8,144,128]{2,1,0:T(8,128)S(1)} all-to-all(f32[8,144,128]{2,1,0:T(8,128)S(1)} %get-tuple-element.16), channel_id=1, replica_groups={{0,2,4,6,8,10,12,14},{1,3,5,7,9,11,13,15},{16,18,20,22,24,26,28,30},{17..., dimensions={0} | all-to-all | bytes 1179648 | tf_op jit(solution)/shard_map/all_to_all | solution.py:457
  26.5 3.3 %collective-permute-start.2 = (f32[1152,128]{1,0:T(8,128)S(1)}, f32[1152,128]{1,0:T(8,128)S(1)}, u32[]{:S(2)}, u32[]{:S(2)}) collective-permute-start(f32[1152,128]{1,0:T(8,128)S(1)} %bitcast.7), channel_id=1, source_target_pairs={{0,1},{1,0},{2,3},{3,2},{4,5},{5,4},{6,7},{7,6},{8,9},{9,8},{10,11... | collective-permute-start | bytes 1769480 | tf_op jit(solution)/shard_map/ppermute | solution.py:461
  29.8 1.6 %collective-permute-done.2.other = f32[1152,128]{1,0:T(8,128)S(1)} collective-permute-done((f32[1152,128]{1,0:T(8,128)S(1)}, f32[1152,128]{1,0:T(8,128)S(1)}, u32[]{:S(2)}, u32[]{:S(2)}) %collective-permute-start.2) | collective-permute-done | bytes 589856 | tf_op jit(solution)/shard_map/ppermute | solution.py:461
  31.5 5.4 %shard_map.78 = f32[256,128]{1,0:T(8,128)S(1)} custom-call(s32[37]{0:T(128)S(1)} %concatenate.7.scalars_of, s32[8,128]{1,0:T(8,128)S(1)} %get-tuple-element.15.ghost_offsets_of, f32[1152,128]{1,0:T(8,128)S(1)} %bitcast.8, f32[1152,128]{1,0:T(8,128)S(1)} %collective-permute-done.2.other), custom_call_target="tpu_custom_call" | custom-call | tf_op jit(solution)/shard_map/pallas_call | solution.py:462
  36.9 10.5 %all_to_all.11 = f32[16,16,128]{2,1,0:T(8,128)S(1)} all-to-all(f32[16,16,128]{2,1,0:T(8,128)S(1)} %bitcast.9), channel_id=1, replica_groups=mesh['gx'=16,'gy'=16] {'gy'}, dimensions={0} | all-to-all | bytes 262144 | tf_op jit(solution)/shard_map/all_to_all | solution.py:470
  47.4 0.7 %shard_map.79 = (f32[2,16,128]{2,1,0:T(8,128)}, f32[3,2,16,128]{3,2,1,0:T(8,128)}, f32[3,2,16,128]{3,2,1,0:T(8,128)}) custom-call(f32[256,128]{1,0:T(8,128)S(1)} %bitcast.10), custom_call_target="tpu_custom_call" | custom-call | tf_op jit(solution)/shard_map/pallas_call | solution.py:473
  (1 shorter events, 0.0 us)
Async XLA Ops:
  0.6 0.8 %copy-start = (s32[2,16]{1,0:T(2,128)S(1)}, s32[2,16]{1,0:T(2,128)}, u32[]{:S(2)}) copy-start(s32[2,16]{1,0:T(2,128)} %offsets.1) | copy-start | bytes 388
  1.5 8.8 %collective-permute-start = (f32[72,128]{1,0:T(8,128)S(1)}, f32[72,128]{1,0:T(8,128)S(1)}, u32[]{:S(2)}, u32[]{:S(2)}) collective-permute-start(f32[72,128]{1,0:T(8,128)S(1)} %get-tuple-element.10), channel_id=1, source_target_pairs={{0,16},{16,32},{32,48},{48,64},{64,80},{80,96},{96,112},{112,128},... | collective-permute-start | bytes 110600 | tf_op jit(solution)/shard_map/ppermute | solution.py:441
  4.0 6.1 %collective-permute-start.1 = (f32[64,128]{1,0:T(8,128)S(1)}, f32[64,128]{1,0:T(8,128)S(1)}, u32[]{:S(2)}, u32[]{:S(2)}) collective-permute-start(f32[64,128]{1,0:T(8,128)S(1)} %get-tuple-element.11), channel_id=1, source_target_pairs={{16,0},{32,16},{48,32},{64,48},{80,64},{96,80},{112,96},{128,112},... | collective-permute-start | bytes 98312 | tf_op jit(solution)/shard_map/ppermute | solution.py:442
  9.2 0.7 %copy-start.1 = (s32[2]{0:T(128)S(1)}, s32[2]{0:T(128)}, u32[]{:S(2)}) copy-start(s32[2]{0:T(128)} %param.9) | copy-start | bytes 28
  26.5 4.9 %collective-permute-start.2 = (f32[1152,128]{1,0:T(8,128)S(1)}, f32[1152,128]{1,0:T(8,128)S(1)}, u32[]{:S(2)}, u32[]{:S(2)}) collective-permute-start(f32[1152,128]{1,0:T(8,128)S(1)} %bitcast.7), channel_id=1, source_target_pairs={{0,1},{1,0},{2,3},{3,2},{4,5},{5,4},{6,7},{7,6},{8,9},{9,8},{10,11... | collective-permute-start | bytes 1769480 | tf_op jit(solution)/shard_map/ppermute | solution.py:461
